TPU v7x, 512 devices: a whole 4x4x16 slice. The times are simulated.
512 devices in a mesh: dp: 64 (over z, x), tensor: 8 (over y, core).
Axes of the slice: x: 4, y: 4, z: 16, core: 2. Of those that a mesh axis runs over, the one named last changes fastest.
Arguments:
- queries: bfloat16 [16384, 4096], P('dp', 'tensor'), may hold values from -8 to 8
- neighbour_keys: bfloat16 [512, 128, 4096], P('dp', None, 'tensor'), may hold values from -8 to 8
- neighbour_values: bfloat16 [512, 128, 4096], P('dp', None, 'tensor'), may hold values from -6 to 6
- residual: bfloat16 [16384, 4096], P(('dp', 'tensor')), may hold values from -1.5 to 1.5
- out_weight: bfloat16 [4096, 4096], P('tensor', 'dp'), may hold values from -0.09375 to 0.09375
- drop_mask: int32 [16384, 4096], P(('dp', 'tensor')), may hold values 0 or 1
- norm_gain: float32 [4096], replicated, may hold values from 0.5 to 1.5
- norm_bias: float32 [4096], replicated, may hold values from -0.5 to 0.5
- neighbour_owner: int32 [256, 2], P('dp'), may hold values from 0 to 63, as said below
- neighbour_slot: int32 [256, 2], P('dp'), may hold values from 0 to 7, as said below
Outputs:
- residual_next: bfloat16 [16384, 4096], P(('dp', 'tensor'))
- layer_normed: bfloat16 [16384, 4096], P(('dp', 'tensor'))
Inputs may be any that keep to these rules, and one draw needn't show every extreme that they name: `neighbour_owner`: the 8 neighbours of the blocks of one dp index are stored on 8 different devices. A device receives at most 12 of all blocks' neighbour requests, and some device exactly that many. `neighbour_slot`: several blocks may use the same stored row.
All inputs are finite; a program needn't handle non-finite values. No bound on the sum of `drop_mask` on one device may be relied on, other than what follows from the above.
Results may differ from a plain program's by a relative error of at most 0.017.
Values may be sent and summed in bfloat16 or wider, within the bound.
A program may use at most 64 MiB of HBM per device.

v0:
```python
import math

import jax
import jax.numpy as jnp
from jax import lax
from jax.sharding import PartitionSpec as P

HEAD = 128


keep_rate = 0.9
norm_eps = 1e-05


def shifted(x, axis, by):
    count = lax.axis_size(axis)
    pairs = [(i, i + by) for i in range(count) if 0 <= i + by < count]
    return lax.ppermute(x, axis, pairs)


def attend_block(query_rows, key_rows, value_rows):
    count_b, count_r, row_width = query_rows.shape
    length = key_rows.shape[1]
    heads_here = row_width // HEAD
    query_heads = query_rows.reshape(count_b, count_r, heads_here, HEAD)
    key_heads = key_rows.reshape(count_b, length, heads_here, HEAD)
    value_heads = value_rows.reshape(count_b, length, heads_here, HEAD)
    scores = jnp.einsum(
        "brhe,blhe->bhrl", query_heads, key_heads, preferred_element_type=jnp.float32
    ) * HEAD ** (-0.5)
    peak_rows = jnp.max(scores, axis=-1)
    raised = jnp.exp(scores - peak_rows[..., None])
    totals = jnp.sum(raised, axis=-1)
    weights = (raised / totals[..., None]).astype(jnp.bfloat16)
    partial_value = jnp.einsum(
        "bhrl,blhe->brhe", weights, value_heads, preferred_element_type=jnp.float32
    )
    partial_value = partial_value.astype(jnp.bfloat16).reshape(count_b, count_r, row_width)
    return (partial_value, jnp.transpose(peak_rows, (0, 2, 1)), jnp.transpose(totals, (0, 2, 1)))


def merge_pair(partials, peak_rows, totals):
    highest = jnp.max(peak_rows, axis=1, keepdims=True)
    merge_weight = totals * jnp.exp(peak_rows - highest)
    weight_sum = jnp.sum(merge_weight, axis=1)
    part_shape = partials.shape
    part_heads = partials.reshape(part_shape[0], part_shape[1], part_shape[2], -1, HEAD).astype(
        jnp.float32
    )
    combined = jnp.sum(part_heads * merge_weight[..., None], axis=1) / weight_sum[..., None]
    return combined.reshape(part_shape[0], part_shape[2], part_shape[3]).astype(jnp.bfloat16)


def local(
    queries,
    neighbour_keys,
    neighbour_values,
    residual,
    out_weight,
    drop_mask,
    norm_gain,
    norm_bias,
    neighbour_owner,
    neighbour_slot,
):
    peer_count = lax.axis_size("dp")
    row_width = queries.shape[1]
    capacity = neighbour_keys.shape[0]
    blocks = neighbour_owner.shape[0]
    span_len = queries.shape[0] // blocks
    carried = shifted(queries[-1:], "dp", 1)
    block_queries = jnp.concatenate([carried, queries[:-1]], axis=0).reshape(
        blocks, span_len, row_width
    )
    owners = neighbour_owner.reshape(-1)
    slot_rows = neighbour_slot.reshape(-1)
    pair_count = owners.shape[0]
    per_block = pair_count // blocks
    peer_ids = jnp.arange(peer_count, dtype=jnp.int32)
    selector = owners[None, :] == peer_ids[:, None]
    repeated = jnp.repeat(block_queries, per_block, axis=0)
    outgoing = jnp.einsum(
        "pn,ncw->pcw", selector.astype(jnp.bfloat16), repeated, preferred_element_type=jnp.float32
    ).astype(jnp.bfloat16)
    wanted = jnp.sum(jnp.where(selector, slot_rows[None, :] + 1, 0), axis=1) - 1
    wanted_rows = jnp.broadcast_to(wanted[:, None], (peer_count, span_len))
    asked_rows = lax.all_to_all(outgoing, "dp", split_axis=0, concat_axis=0, tiled=True)
    asked_slot = lax.all_to_all(wanted_rows, "dp", split_axis=0, concat_axis=0, tiled=True)
    peer_slot = jnp.max(asked_slot, axis=1, initial=-1)
    chosen = jnp.clip(peer_slot, 0, capacity - 1)
    group_size = math.gcd(peer_count, 16)
    rounds = peer_count // group_size

    def one_group(group_items):
        group_rows, group_slots = group_items
        return attend_block(
            group_rows,
            jnp.take(neighbour_keys, group_slots, axis=0),
            jnp.take(neighbour_values, group_slots, axis=0),
        )

    results = lax.map(
        one_group,
        (
            asked_rows.reshape((rounds, group_size) + asked_rows.shape[1:]),
            chosen.reshape(rounds, group_size),
        ),
    )
    part_answer = results[0].reshape((peer_count,) + results[0].shape[2:])
    peak_answer = results[1].reshape((peer_count,) + results[1].shape[2:])
    total_answer = results[2].reshape((peer_count,) + results[2].shape[2:])
    part_back = lax.all_to_all(part_answer, "dp", split_axis=0, concat_axis=0, tiled=True)
    own_partial = jnp.take(part_back, owners, axis=0).reshape(
        blocks, per_block, span_len, row_width
    )
    own_peak = jnp.take(
        lax.all_to_all(peak_answer, "dp", split_axis=0, concat_axis=0, tiled=True), owners, axis=0
    ).reshape(blocks, per_block, span_len, -1)
    own_total = jnp.take(
        lax.all_to_all(total_answer, "dp", split_axis=0, concat_axis=0, tiled=True), owners, axis=0
    ).reshape(blocks, per_block, span_len, -1)
    merged = merge_pair(own_partial, own_peak, own_total)
    flat_rows = merged.reshape(-1, row_width)
    following = shifted(flat_rows[:1], "dp", -1)
    cross_rows = jnp.concatenate([flat_rows[1:], following], axis=0)
    whole_weight = lax.all_gather(out_weight, "dp", axis=1, tiled=True)
    branch = lax.psum_scatter(
        jnp.dot(cross_rows, whole_weight, preferred_element_type=jnp.float32).astype(jnp.bfloat16),
        "tensor",
        scatter_dimension=0,
        tiled=True,
    ).astype(jnp.float32)
    keep_scale = drop_mask.astype(jnp.float32) * (1.0 / keep_rate)
    stream = residual.astype(jnp.float32) + keep_scale * branch
    centre = jnp.mean(stream, axis=1, keepdims=True)
    spread = jnp.mean(jnp.square(stream - centre), axis=1, keepdims=True)
    normed = (stream - centre) * lax.rsqrt(spread + norm_eps) * norm_gain + norm_bias
    return (stream.astype(jnp.bfloat16), normed.astype(jnp.bfloat16))


def solution(mesh):
    placed = (
        P("dp", "tensor"),
        P("dp", None, "tensor"),
        P("dp", None, "tensor"),
        P(("dp", "tensor"), None),
        P("tensor", "dp"),
        P(("dp", "tensor"), None),
        P(),
        P(),
        P("dp", None),
        P("dp", None),
    )
    return jax.shard_map(
        local,
        mesh=mesh,
        in_specs=placed,
        out_specs=(P(("dp", "tensor"), None), P(("dp", "tensor"), None)),
        check_vma=False,
    )
```

profile of v0, /device:TPU:1, one launch (start us, length us, event | category | flops | bytes accessed | tf_op | source)
XLA Modules:
  0.0 645.2 jit_solution(470251790129290026)
XLA Ops:
  7.9 3.9 collective-permute-start
  14.4 18.0 %all-to-all-start = ((s32[64,1,64]{2,1,0:T(1,128)}), s32[64,1,64]{2,1,0:T(1,128)S(1)}, u32[]{:S(2)}, u32[]{:S(2)}) async-start(s32[64,1,64]{2,1,0:T(1,128)} %broadcast_in_dim.77), calls=%async_computation | async-start | bytes 65536 | tf_op jit(solution)/shard_map/all_to_all | solution.py:88
  32.4 1.0 pad_maximum_fusion
  34.1 1.4 convolution_convert_fusion.1
  35.5 4.4 copy.65
  39.9 5.9 all-to-all-done
  45.8 9.1 %all-to-all-start.1 = ((bf16[64,64,512]{2,1,0:T(8,128)(2,1)}), bf16[64,64,512]{2,1,0:T(8,128)(2,1)}, u32[]{:S(2)}, u32[]{:S(2)}) async-start(bf16[64,64,512]{2,1,0:T(8,128)(2,1)} %copy.65), calls=%async_computation.1 | async-start | bytes 8388608 | tf_op jit(solution)/shard_map/all_to_all | solution.py:87
  55.1 183.1 %all-to-all-done.1 = bf16[64,64,512]{2,1,0:T(8,128)(2,1)} async-done(((bf16[64,64,512]{2,1,0:T(8,128)(2,1)}), bf16[64,64,512]{2,1,0:T(8,128)(2,1)}, u32[]{:S(2)}, u32[]{:S(2)}) %all-to-all-start.1) | async-done | bytes 4194336 | tf_op jit(solution)/shard_map/all_to_all | solution.py:87
  238.1 85.8 %while.14 = (s32[]{:T(128)}, bf16[4,16,64,512]{3,2,1,0:T(8,128)(2,1)}, f32[4,16,64,4]{2,3,1,0:T(4,128)S(1)}, f32[4,16,64,4]{2,3,1,0:T(4,128)S(1)}, s32[4,16]{1,0...) while((s32[]{:T(128)}, ...), condition=%wide.region_5.7_spmd, body=%wide.region_2.6_spmd.sunk | while | flops 275768416 | bytes 56841260 | solution.py:102
  238.2 2.0 gather_fusion
  240.2 2.0 gather_fusion.1
  242.2 4.0 select_bitcast_fusion.3
  246.2 2.3 constant_dynamic-slice_fusion.3
  248.5 1.3 reshape.230
  249.9 1.7 multiply_reduce_fusion.4
  251.6 1.3 fusion.38
  253.2 1.9 fusion.39
  255.0 1.8 copy.99
  256.9 1.6 broadcast_in_dim.119
  258.5 1.2 constant_dynamic-update-slice_fusion.2
  259.7 2.0 gather_fusion
  261.7 2.0 gather_fusion.1
  263.8 4.0 select_bitcast_fusion.3
  267.8 2.3 constant_dynamic-slice_fusion.3
  270.1 1.3 reshape.230
  271.4 1.6 multiply_reduce_fusion.4
  273.1 1.3 fusion.38
  274.7 1.9 fusion.39
  276.5 1.8 copy.99
  278.4 1.6 broadcast_in_dim.119
  280.0 1.1 constant_dynamic-update-slice_fusion.2
  281.1 2.0 gather_fusion
  283.2 2.0 gather_fusion.1
  285.2 4.0 select_bitcast_fusion.3
  289.2 2.3 constant_dynamic-slice_fusion.3
  291.5 1.3 reshape.230
  292.9 1.7 multiply_reduce_fusion.4
  294.5 1.3 fusion.38
  296.1 1.9 fusion.39
  298.0 1.8 copy.99
  299.8 1.6 broadcast_in_dim.119
  301.4 1.1 constant_dynamic-update-slice_fusion.2
  302.6 2.0 gather_fusion
  304.6 2.0 gather_fusion.1
  306.6 4.0 select_bitcast_fusion.3
  310.6 2.3 constant_dynamic-slice_fusion.3
  312.9 1.3 reshape.230
  314.3 1.6 multiply_reduce_fusion.4
  316.0 1.3 fusion.38
  317.5 1.9 fusion.39
  319.4 1.8 copy.99
  321.3 1.6 broadcast_in_dim.119
  322.9 1.1 constant_dynamic-update-slice_fusion.2
  324.7 11.7 %all-to-all-start.4 = ((f32[64,1,256]{2,1,0:T(1,128)}), f32[64,1,256]{2,1,0:T(1,128)S(1)}, u32[]{:S(2)}, u32[]{:S(2)}) async-start(f32[64,1,256]{2,1,0:T(1,128)} %reshape.219), calls=%async_computation.4 | async-start | bytes 131072 | tf_op jit(solution)/shard_map/all_to_all | solution.py:117
  336.5 13.9 %all-to-all-done.4 = f32[64,1,256]{2,1,0:T(1,128)S(1)} async-done(((f32[64,1,256]{2,1,0:T(1,128)}), f32[64,1,256]{2,1,0:T(1,128)S(1)}, u32[]{:S(2)}, u32[]{:S(2)}) %all-to-all-start.4) | async-done | bytes 65568 | tf_op jit(solution)/shard_map/all_to_all | solution.py:117
  350.4 17.8 %all_to_all.26 = f32[64,1,256]{2,1,0:T(1,128)S(1)} all-to-all(f32[64,1,256]{2,1,0:T(1,128)S(1)} %reshape.217), channel_id=1, replica_groups=mesh['dp'=64,'tensor'=8] {'dp'}, dimensions={0} | all-to-all | bytes 131072 | tf_op jit(solution)/shard_map/all_to_all | solution.py:120
  368.2 5.8 all-to-all-start.2
  379.0 196.2 %all-to-all-done.2 = bf16[64,64,512]{2,1,0:T(8,128)(2,1)} async-done(((bf16[64,64,512]{2,1,0:T(8,128)(2,1)}), bf16[64,64,512]{2,1,0:T(8,128)(2,1)}, u32[]{:S(2)}, u32[]{:S(2)}) %all-to-all-start.2) | async-done | bytes 4194336 | tf_op jit(solution)/shard_map/all_to_all | solution.py:112
  575.2 2.8 gather_fusion.2
  579.4 1.3 collective-permute-start.1
  580.8 8.6 %all-gather.2.cloned.1.call-done = bf16[512,4096]{0,1:T(8,128)(2,1)} async-done(((bf16[512,64]{0,1:T(8,128)(2,1)}), bf16[512,4096]{0,1:T(8,128)(2,1)}) %all-gather.2.cloned.1.call-update) | async-done | bytes 4194320 | tf_op jit(solution)/shard_map/all_gather | solution.py:126
  589.5 4.8 convolution_convert_fusion
  594.3 41.6 %reduce-scatter.2.cloned.1.call-done = bf16[32,4096]{1,0:T(8,128)(2,1)} async-done(((bf16[256,4096]{1,0:T(8,128)(2,1)}), bf16[32,4096]{1,0:T(8,128)(2,1)}) %reduce-scatter.2.cloned.1.call-update) | async-done | bytes 262160 | tf_op jit(solution)/shard_map/reduce_scatter | solution.py:127
  635.9 1.2 fusion.29
  (105 shorter events, 13.7 us)
Async XLA Ops:
  7.9 24.5 %collective-permute-start = (bf16[1,512]{1,0:T(2,128)(2,1)S(1)}, bf16[1,512]{1,0:T(2,128)(2,1)S(1)}, u32[]{:S(2)}, u32[]{:S(2)}) collective-permute-start(bf16[1,512]{1,0:T(2,128)(2,1)S(1)} %slice.12), channel_id=1, source_target_pairs={{0,8},{8,16},{16,24},{24,32},{32,40},{40,48},{48,56},{56,64},{64,7... | collective-permute-start | bytes 3080 | tf_op jit(solution)/shard_map/ppermute | solution.py:18
  14.4 31.4 %all-to-all-start = ((s32[64,1,64]{2,1,0:T(1,128)}), s32[64,1,64]{2,1,0:T(1,128)S(1)}, u32[]{:S(2)}, u32[]{:S(2)}) async-start(s32[64,1,64]{2,1,0:T(1,128)} %broadcast_in_dim.77), calls=%async_computation | async-start | bytes 65536 | tf_op jit(solution)/shard_map/all_to_all | solution.py:88
  39.9 198.3 %copy-start = (bf16[8,128,512]{2,1,0:T(8,128)(2,1)S(1)}, bf16[8,128,512]{2,1,0:T(8,128)(2,1)}, u32[]{:S(2)}) copy-start(bf16[8,128,512]{2,1,0:T(8,128)(2,1)} %param.18) | copy-start | bytes 3145732
  39.9 198.3 %copy-start.2 = (bf16[8,128,512]{2,1,0:T(8,128)(2,1)S(1)}, bf16[8,128,512]{2,1,0:T(8,128)(2,1)}, u32[]{:S(2)}) copy-start(bf16[8,128,512]{2,1,0:T(8,128)(2,1)} %param.17) | copy-start | bytes 3145732
  45.8 192.4 %all-to-all-start.1 = ((bf16[64,64,512]{2,1,0:T(8,128)(2,1)}), bf16[64,64,512]{2,1,0:T(8,128)(2,1)}, u32[]{:S(2)}, u32[]{:S(2)}) async-start(bf16[64,64,512]{2,1,0:T(8,128)(2,1)} %copy.65), calls=%async_computation.1 | async-start | bytes 8388608 | tf_op jit(solution)/shard_map/all_to_all | solution.py:87
  251.6 1.6 copy-start.4
  256.9 2.8 copy-start.1
  256.9 2.8 copy-start.3
  273.1 1.6 copy-start.4
  278.4 2.7 copy-start.1
  278.4 2.7 copy-start.3
  294.5 1.6 copy-start.4
  299.8 2.7 copy-start.1
  299.8 2.7 copy-start.3
  315.9 1.6 copy-start.4
  321.3 2.7 copy-start.1
  321.3 2.7 copy-start.3
  324.7 25.7 %all-to-all-start.4 = ((f32[64,1,256]{2,1,0:T(1,128)}), f32[64,1,256]{2,1,0:T(1,128)S(1)}, u32[]{:S(2)}, u32[]{:S(2)}) async-start(f32[64,1,256]{2,1,0:T(1,128)} %reshape.219), calls=%async_computation.4 | async-start | bytes 131072 | tf_op jit(solution)/shard_map/all_to_all | solution.py:117
  368.2 6.7 %copy-start.9 = (s32[4,2]{0,1:T(2,128)S(1)}, s32[4,2]{0,1:T(2,128)}, u32[]{:S(2)}) copy-start(s32[4,2]{0,1:T(2,128)} %param.24) | copy-start | bytes 100
  368.2 207.0 %all-to-all-start.2 = ((bf16[64,64,512]{2,1,0:T(8,128)(2,1)}), bf16[64,64,512]{2,1,0:T(8,128)(2,1)}, u32[]{:S(2)}, u32[]{:S(2)}) async-start(bf16[64,64,512]{2,1,0:T(8,128)(2,1)} %bitcast.78), calls=%async_computation.2 | async-start | bytes 8388608 | tf_op jit(solution)/shard_map/all_to_all | solution.py:112
  374.0 215.4 %all-gather.2.cloned.1.call-start = ((), (), s32[]{:S(2)}) async-start(), calls=%async_computation.6 | async-start | bytes 4259840 | tf_op jit(solution)/shard_map/all_gather | solution.py:126
  374.8 261.2 %reduce-scatter.2.cloned.1.call-start = ((), (), s32[]{:S(2)}) async-start(), calls=%async_computation.7 | async-start | bytes 2359296 | tf_op jit(solution)/shard_map/reduce_scatter | solution.py:127
  579.4 10.0 %collective-permute-start.1 = (bf16[1,512]{1,0:T(2,128)(2,1)S(1)}, bf16[1,512]{1,0:T(2,128)(2,1)S(1)}, u32[]{:S(2)}, u32[]{:S(2)}) collective-permute-start(bf16[1,512]{1,0:T(2,128)(2,1)S(1)} %slice.27), channel_id=1, source_target_pairs={{8,0},{16,8},{24,16},{32,24},{40,32},{48,40},{56,48},{64,56},{72,6... | collective-permute-start | bytes 3080 | tf_op jit(solution)/shard_map/ppermute | solution.py:18
  594.3 41.7 %copy-start.5 = (s32[32,4096]{1,0:T(8,128)S(1)}, s32[32,4096]{1,0:T(8,128)}, u32[]{:S(2)}) copy-start(s32[32,4096]{1,0:T(8,128)} %param.21) | copy-start | bytes 1572868
  594.3 41.7 %copy-start.6 = (bf16[32,4096]{1,0:T(8,128)(2,1)S(1)}, bf16[32,4096]{1,0:T(8,128)(2,1)}, u32[]{:S(2)}) copy-start(bf16[32,4096]{1,0:T(8,128)(2,1)} %param.19) | copy-start | bytes 786436
  594.3 43.1 %copy-start.7 = (f32[4096]{0:T(1024)S(1)}, f32[4096]{0:T(1024)}, u32[]{:S(2)}) copy-start(f32[4096]{0:T(1024)} %param.23) | copy-start | bytes 49156
  594.3 43.1 %copy-start.8 = (f32[4096]{0:T(1024)S(1)}, f32[4096]{0:T(1024)}, u32[]{:S(2)}) copy-start(f32[4096]{0:T(1024)} %param.22) | copy-start | bytes 49156
Sparse Core Ops, SparseCore 0:
  377.8 211.6 all-gather.1
  594.4 41.4 reduce-scatter.1
where the time goes:
time: 647 us; the launch traced here: 645 us
  waiting for transfers between devices  450 us (70%)
  local copies, waits for them, and re-layouts  64.1 us (10%)
  starting transfers between devices  49.8 us (8%)
  other arithmetic  28.7 us (4%)
  matrix products  20.2 us (3%)
  blocking collectives  17.8 us (3%)
  between operations  14.3 us (2%)
    all_to_all x1, waiting for transfers between devices, local(): lax.all_to_all(part_answer, 'dp', split_axis=0, concat_axis=0, tiled=True)  196 us
    all_to_all x1, waiting for transfers between devices, local(): lax.all_to_all(outgoing, 'dp', split_axis=0, concat_axis=0, tiled=True)  183 us
    reduce_scatter x1, waiting for transfers between devices, local(): lax.psum_scatter(jnp.dot(cross_rows, whole_weight, preferred_element_type...  41.6 us
    all_to_all x1, starting transfers between devices, local(): lax.all_to_all(wanted_rows, 'dp', split_axis=0, concat_axis=0, tiled=True)  18 us
    all_to_all x1, blocking collectives, local(): lax.all_to_all(total_answer, 'dp', split_axis=0, concat_axis=0, tiled=True)  17.8 us
    while x4, other arithmetic  16 us
    all_to_all x1, waiting for transfers between devices, local(): lax.all_to_all(peak_answer, 'dp', split_axis=0, concat_axis=0, tiled=True)  13.9 us
  transfers between devices with their start and end apart: 8, of which 6 were waited for; matrix products, arithmetic and copies ran while one was open for 3% of the time, Pallas kernels for 0%

commit v1 on v0

v1 whole, which is shorter than its diff:
```python
import functools

import jax
import jax.numpy as jnp
from jax import lax
from jax.experimental import pallas as pl
from jax.experimental.pallas import tpu as pltpu
from jax.sharding import PartitionSpec as P

HEAD = 128
XN = 4
CAP = 12
HALF = CAP // 2
SROWS = 16
GROUP = 2
NONE = -1e30

keep_rate = 0.9
norm_eps = 1e-05
MESH = pl.DeviceIdType.MESH


def shifted(x, axis, by):
    count = lax.axis_size(axis)
    pairs = [(i, i + by) for i in range(count) if 0 <= i + by < count]
    return lax.ppermute(x, axis, pairs)


def routing_tables(owner, slot, capacity):
    blocks, nbrs = owner.shape
    per = blocks * nbrs
    me = lax.axis_index("dp")
    z, x = me // XN, me % XN
    code = (owner * capacity + slot).reshape(per)
    every = lax.all_gather(code, "dp", axis=0, tiled=True)
    count = every.shape[0]
    zn = count // per // XN
    own = every // capacity
    row = every % capacity
    i = jnp.arange(count, dtype=jnp.int32)
    src = i // per
    z0, x0 = src // XN, src % XN
    block = z0 * blocks + (i // nbrs) % blocks
    rank = jnp.sum(
        ((own[None, :] == own[:, None]) & (i[None, :] < i[:, None])).astype(jnp.int32), axis=1
    )
    j = jnp.arange(CAP, dtype=jnp.int32)
    rel = jnp.arange(XN, dtype=jnp.int32)
    target = z * XN + (x + rel) % XN
    hit = (
        (own[None, None, :] == target[:, None, None])
        & (rank[None, None, :] == j[None, :, None])
        & (x0[None, None, :] == x)
    )
    pick = jnp.max(jnp.where(hit, block[None, None, :], -1), axis=-1)
    mine = (own[None, :] == me) & (rank[None, :] == j[:, None])
    store = jnp.max(jnp.where(mine, row[None, :], 0), axis=-1)
    back = (x0[None, :] - x + XN) % XN
    way = jnp.where(
        back == 0,
        0,
        jnp.where(
            back == 3,
            1,
            jnp.where(back == 1, 2, jnp.where(j[:, None] < HALF, 1, 2)),
        ),
    )
    path = jnp.max(jnp.where(mine, way, 0), axis=-1)
    col_own = lax.dynamic_index_in_dim(own.reshape(zn, XN, per), x, 1, keepdims=False)
    col_rank = lax.dynamic_index_in_dim(rank.reshape(zn, XN, per), x, 1, keepdims=False)
    here = (col_own // XN) == z
    place = (col_own % XN - x + XN) % XN
    data_at = jnp.where(here, place * CAP + col_rank, 0)
    stat_at = jnp.where(here, place * SROWS + col_rank, CAP)
    return jnp.concatenate(
        [pick.reshape(-1), store, path, data_at.reshape(-1), stat_at.reshape(-1)]
    ).astype(jnp.int32)


def route_kernel(zn, blocks, tab, q_ref, k_ref, v_ref, out_ref, *scratch):
    groups = q_ref.shape[0]
    span = q_ref.shape[2]
    wide = q_ref.shape[3]
    me = lax.axis_index("dp")
    tens = lax.axis_index("tensor")
    z, x = me // XN, me % XN
    z_up = ((z + 1) % zn) * XN + x
    z_dn = ((z + zn - 1) % zn) * XN + x
    x_up = z * XN + (x + 1) % XN
    x_dn = z * XN + (x + XN - 1) % XN
    per_g = 11
    bufs = [scratch[g * per_g : (g + 1) * per_g] for g in range(groups)]
    (
        lse_acc,
        w_scr,
        ag_send,
        ag_recv,
        x_send,
        x_recv,
        rd_send,
        rd_recv,
        rs_send,
        rs_recv,
    ) = scratch[groups * per_g :]
    PICK, STORE, PATH = 0, XN * CAP, XN * CAP + CAP
    DATA = XN * CAP + 2 * CAP
    STAT = DATA + zn * blocks * 2
    hb = blocks // 2
    chains = [(1, 0, zn // 2), (1, 1, zn // 2 - 1), (-1, 0, zn // 2 - 1), (-1, 1, zn // 2)]
    started = []

    barrier = pltpu.get_barrier_semaphore()
    for peer in (z_up, z_dn, x_up, x_dn):
        pl.semaphore_signal(barrier, inc=1, device_id=(peer, tens), device_id_type=MESH)
    pl.semaphore_wait(barrier, 4)

    def remote(src, dst, send, recv, peer):
        copy = pltpu.make_async_remote_copy(
            src_ref=src,
            dst_ref=dst,
            send_sem=send,
            recv_sem=recv,
            device_id=(peer, tens),
            device_id_type=MESH,
        )
        copy.start()
        started.append(copy)
        return copy

    def gather(g):
        col = bufs[g][0]
        for b in range(blocks):
            col[z * blocks + b] = q_ref[g, b]
        for s in range(zn // 2 + 1):
            for c, (way, half, steps) in enumerate(chains):
                if s > steps:
                    continue
                at = ((z - way * s + zn) % zn) * blocks + half * hb
                here = col.at[pl.ds(at, hb)]
                if s > 0:
                    pltpu.make_async_remote_copy(
                        src_ref=here,
                        dst_ref=here,
                        send_sem=ag_send.at[g, c, s - 1],
                        recv_sem=ag_recv.at[g, c, s - 1],
                        device_id=(z_up, tens),
                        device_id_type=MESH,
                    ).wait_recv()
                if s < steps:
                    src = q_ref.at[g, pl.ds(half * hb, hb)] if s == 0 else here
                    remote(
                        src,
                        here,
                        ag_send.at[g, c, s],
                        ag_recv.at[g, c, s],
                        z_up if way > 0 else z_dn,
                    )
            yield

    def exchange(g):
        col, s1r, s1l, a1l, a1r, s2, a2, res, stat, _, _ = bufs[g]

        def pick(rel, j):
            return col[jnp.maximum(tab[PICK + rel * CAP + j], 0)]

        def asked(rel, j):
            return tab[PICK + rel * CAP + j] >= 0

        @pl.loop(0, HALF)
        def _(j):
            s1r[j] = pick(2, j)
            s1l[j] = pick(2, j + HALF)

        step1r = remote(s1r, a1l, x_send.at[g, 0], x_recv.at[g, 0], x_up)
        step1l = remote(s1l, a1r, x_send.at[g, 1], x_recv.at[g, 1], x_dn)

        @pl.loop(0, HALF)
        def _(j):
            s2[0, j + HALF] = pick(1, j + HALF)
            s2[1, j] = pick(3, j)

        lo, hi = pl.ds(0, HALF), pl.ds(HALF, HALF)
        step2 = [
            remote(s2.at[0, hi], a2.at[0, hi], x_send.at[g, 2], x_recv.at[g, 2], x_up),
            remote(s2.at[1, lo], a2.at[1, lo], x_send.at[g, 3], x_recv.at[g, 3], x_dn),
        ]
        yield
        step1r.wait_recv()
        step1l.wait_recv()

        @pl.loop(0, HALF)
        def _(j):
            s2[0, j] = jnp.where(asked(1, j), pick(1, j), a1l[j])
            s2[1, j + HALF] = jnp.where(asked(3, j + HALF), pick(3, j + HALF), a1r[j])

        step2 += [
            remote(s2.at[0, lo], a2.at[0, lo], x_send.at[g, 4], x_recv.at[g, 4], x_up),
            remote(s2.at[1, hi], a2.at[1, hi], x_send.at[g, 5], x_recv.at[g, 5], x_dn),
        ]
        yield
        for copy in step2:
            copy.wait_recv()

        lane = lax.broadcasted_iota(jnp.int32, (span, HEAD), 1)

        @pl.loop(0, CAP)
        def _(j):
            path = tab[PATH + j]
            rows = jnp.where(
                path == 0, pick(0, j), jnp.where(path == 1, a2[0, j], a2[1, j])
            )
            at = tab[STORE + j]
            for h in range(GROUP):
                here = slice(h * HEAD, (h + 1) * HEAD)
                cols = slice((g * GROUP + h) * HEAD, (g * GROUP + h + 1) * HEAD)
                scores = lax.dot_general(
                    rows[:, here],
                    k_ref[at, :, cols],
                    (((1,), (1,)), ((), ())),
                    preferred_element_type=jnp.float32,
                ) * HEAD ** (-0.5)
                peak = jnp.max(scores, axis=-1, keepdims=True)
                raised = jnp.exp(scores - peak)
                total = jnp.sum(raised, axis=-1, keepdims=True)
                prob = (raised / total).astype(jnp.bfloat16)
                part = jnp.dot(prob, v_ref[at, :, cols], preferred_element_type=jnp.float32)
                res[j, :, here] = part.astype(jnp.bfloat16)
                old = lse_acc[h * span : (h + 1) * span, :]
                lse_acc[h * span : (h + 1) * span, :] = jnp.where(
                    lane == j, peak + jnp.log(total), old
                )

        turned = jnp.transpose(lse_acc[...])[0:SROWS]
        slot_row = lax.broadcasted_iota(jnp.int32, turned.shape, 0)
        stat[0:SROWS, :] = jnp.where(slot_row < CAP, turned, NONE)

        def part_of(rel, first):
            return res.at[pl.ds(rel * CAP + first, HALF)]

        def stats_of(rel, first=0, rows=SROWS):
            return stat.at[pl.ds(rel * SROWS + first, rows)]

        def send(src, dst, at, peer):
            return remote(src, dst, x_send.at[g, at], x_recv.at[g, at], peer)

        r_lo = send(part_of(0, 0), part_of(3, 0), 6, x_up)
        l_hi = send(part_of(0, HALF), part_of(1, HALF), 7, x_dn)
        r_st = send(stats_of(0), stats_of(3), 8, x_up)
        l_st = send(stats_of(0), stats_of(1), 9, x_dn)
        r_hi = send(part_of(0, HALF), part_of(3, HALF), 10, x_up)
        l_lo = send(part_of(0, 0), part_of(1, 0), 11, x_dn)
        yield
        r_lo.wait_recv()
        f_r = send(part_of(3, 0), part_of(2, 0), 12, x_up)
        l_hi.wait_recv()
        f_l = send(part_of(1, HALF), part_of(2, HALF), 13, x_dn)
        r_st.wait_recv()
        f_rs = send(stats_of(3, 0, 8), stats_of(2, 0, 8), 14, x_up)
        l_st.wait_recv()
        f_ls = send(stats_of(1, 8, 8), stats_of(2, 8, 8), 15, x_dn)
        yield
        for copy in (r_hi, l_lo, f_r, f_l, f_rs, f_ls):
            copy.wait_recv()
        yield

    def combine(g, z0, half, arrived, dst, dst_stat, scr):
        res, stat = bufs[g][7], bufs[g][8]
        count = len(arrived) + 2
        for b in range(hb):
            base = (z0 * blocks + half * hb + b) * 2
            lses = [ref[b : b + 1, :] for _, ref in arrived]
            lses += [stat[pl.ds(tab[STAT + base + r], 1), :] for r in range(2)]
            top = functools.reduce(jnp.maximum, lses)
            weights = [jnp.exp(v - top) for v in lses]
            total = functools.reduce(jnp.add, weights)
            for n, w in enumerate(weights):
                w_scr[scr, b, n : n + 1, :] = w / total
            if dst_stat is not None:
                dst_stat[b : b + 1, :] = top + jnp.log(total)
        for b in range(hb):
            base = (z0 * blocks + half * hb + b) * 2
            cols = jnp.transpose(w_scr[scr, b])
            vals = [ref[b] for ref, _ in arrived]
            vals += [res[tab[DATA + base + r]] for r in range(2)]
            outs = []
            for h in range(GROUP):
                here = slice(h * HEAD, (h + 1) * HEAD)
                w = cols[h * span : (h + 1) * span]
                acc = vals[0][:, here].astype(jnp.float32) * w[:, 0:1]
                for n in range(1, count):
                    acc += vals[n][:, here].astype(jnp.float32) * w[:, n : n + 1]
                outs.append(acc.astype(jnp.bfloat16))
            dst[b] = jnp.concatenate(outs, axis=1)

    def reduce(g):
        ring, ring_stat = bufs[g][9], bufs[g][10]
        for s in range(zn // 2 + 1):
            for c, (way, half, steps) in enumerate(chains):
                i = s - (zn // 2 - steps)
                if i < 0 or i > steps:
                    continue
                here, here_stat = ring.at[c, i], ring_stat.at[c, i]
                peer = z_up if way > 0 else z_dn
                if i > 0:
                    for ref, snd, rcv in (
                        (here, rd_send, rd_recv),
                        (here_stat, rs_send, rs_recv),
                    ):
                        pltpu.make_async_remote_copy(
                            src_ref=ref,
                            dst_ref=ref,
                            send_sem=snd.at[g, c, i - 1],
                            recv_sem=rcv.at[g, c, i - 1],
                            device_id=(peer, tens),
                            device_id_type=MESH,
                        ).wait_recv()
                if i < steps:
                    z0 = (z + way * (steps - i) + zn) % zn
                    arrived = [(here, here_stat)] if i > 0 else []
                    combine(g, z0, half, arrived, here, here_stat, c)
                    remote(
                        here,
                        ring.at[c, i + 1],
                        rd_send.at[g, c, i],
                        rd_recv.at[g, c, i],
                        peer,
                    )
                    remote(
                        here_stat,
                        ring_stat.at[c, i + 1],
                        rs_send.at[g, c, i],
                        rs_recv.at[g, c, i],
                        peer,
                    )
            yield
        for half in range(2):
            arrived = [
                (ring.at[c, steps], ring_stat.at[c, steps])
                for c, (_, part, steps) in enumerate(chains)
                if part == half
            ]
            combine(
                g, z, half, arrived, out_ref.at[g, pl.ds(half * hb, hb)], None, half
            )
        yield

    def weave(first, second):
        live = [iter(first), iter(second)]
        while live:
            live = [it for it in live if next(it, "end") != "end"]

    def run(it):
        for _ in it:
            pass

    run(gather(0))
    for g in range(1, groups):
        weave(gather(g), exchange(g - 1)) if g == 1 else weave(reduce(g - 2), gather(g))
    weave(reduce(groups - 2), exchange(groups - 1))
    run(reduce(groups - 1))
    for copy in started:
        copy.wait_send()


def route(tab, q, k, v):
    groups, blocks, span, wide = q.shape
    zn = lax.axis_size("dp") // XN
    steps = zn // 2
    bf, f32 = jnp.bfloat16, jnp.float32
    per_group = [
        pltpu.VMEM((zn * blocks, span, wide), bf),
        pltpu.VMEM((HALF, span, wide), bf),
        pltpu.VMEM((HALF, span, wide), bf),
        pltpu.VMEM((HALF, span, wide), bf),
        pltpu.VMEM((HALF, span, wide), bf),
        pltpu.VMEM((2, CAP, span, wide), bf),
        pltpu.VMEM((2, CAP, span, wide), bf),
        pltpu.VMEM((XN * CAP, span, wide), bf),
        pltpu.VMEM((XN * SROWS, HEAD), f32),
        pltpu.VMEM((4, steps + 1, blocks // 2, span, wide), bf),
        pltpu.VMEM((4, steps + 1, 8, HEAD), f32),
    ]
    dma = pltpu.SemaphoreType.DMA
    vmem = pl.BlockSpec(memory_space=pltpu.VMEM)
    return pl.pallas_call(
        functools.partial(route_kernel, zn, blocks),
        out_shape=jax.ShapeDtypeStruct(q.shape, bf),
        in_specs=[pl.BlockSpec(memory_space=pltpu.SMEM), vmem, vmem, vmem],
        out_specs=vmem,
        scratch_shapes=per_group * groups
        + [
            pltpu.VMEM((GROUP * span, HEAD), f32),
            pltpu.VMEM((4, 2, 8, HEAD), f32),
            dma((groups, 4, steps)),
            dma((groups, 4, steps)),
            dma((groups, 16)),
            dma((groups, 16)),
            dma((groups, 4, steps)),
            dma((groups, 4, steps)),
            dma((groups, 4, steps)),
            dma((groups, 4, steps)),
        ],
        compiler_params=pltpu.CompilerParams(
            collective_id=0, has_side_effects=True, vmem_limit_bytes=48 * 1024 * 1024
        ),
        cost_estimate=pl.CostEstimate(
            flops=400_000_000, bytes_accessed=16_000_000, transcendentals=400_000
        ),
    )(tab, q, k, v)


def local(
    queries,
    neighbour_keys,
    neighbour_values,
    residual,
    out_weight,
    drop_mask,
    norm_gain,
    norm_bias,
    neighbour_owner,
    neighbour_slot,
):
    row_width = queries.shape[1]
    blocks = neighbour_owner.shape[0]
    span = queries.shape[0] // blocks
    wide = GROUP * HEAD
    groups = row_width // wide
    tab = routing_tables(neighbour_owner, neighbour_slot, neighbour_keys.shape[0])
    carried = shifted(queries[-1:], "dp", 1)
    asked = jnp.concatenate([carried, queries[:-1]], axis=0)
    asked = asked.reshape(blocks, span, groups, wide).transpose(2, 0, 1, 3)
    merged = route(tab, asked, neighbour_keys, neighbour_values)
    flat_rows = merged.transpose(1, 2, 0, 3).reshape(-1, row_width)
    following = shifted(flat_rows[:1], "dp", -1)
    cross_rows = jnp.concatenate([flat_rows[1:], following], axis=0)
    whole_weight = lax.all_gather(out_weight, "dp", axis=1, tiled=True)
    branch = lax.psum_scatter(
        jnp.dot(cross_rows, whole_weight, preferred_element_type=jnp.float32).astype(jnp.bfloat16),
        "tensor",
        scatter_dimension=0,
        tiled=True,
    ).astype(jnp.float32)
    keep_scale = drop_mask.astype(jnp.float32) * (1.0 / keep_rate)
    stream = residual.astype(jnp.float32) + keep_scale * branch
    centre = jnp.mean(stream, axis=1, keepdims=True)
    spread = jnp.mean(jnp.square(stream - centre), axis=1, keepdims=True)
    normed = (stream - centre) * lax.rsqrt(spread + norm_eps) * norm_gain + norm_bias
    return (stream.astype(jnp.bfloat16), normed.astype(jnp.bfloat16))


def solution(mesh):
    placed = (
        P("dp", "tensor"),
        P("dp", None, "tensor"),
        P("dp", None, "tensor"),
        P(("dp", "tensor"), None),
        P("tensor", "dp"),
        P(("dp", "tensor"), None),
        P(),
        P(),
        P("dp", None),
        P("dp", None),
    )
    return jax.shard_map(
        local,
        mesh=mesh,
        in_specs=placed,
        out_specs=(P(("dp", "tensor"), None), P(("dp", "tensor"), None)),
        check_vma=False,
    )
```

time: 647 us -> 299 us (0.46)
  waiting for transfers between devices: 450 us -> 65 us
  Pallas kernels: 0 us -> 167 us
  local copies, waits for them, and re-layouts: 64.1 us -> 6.03 us
  starting transfers between devices: 49.8 us -> 5.3 us
  other arithmetic: 28.7 us -> 5.04 us
  matrix products: 20.2 us -> 4.81 us
  blocking collectives: 17.8 us -> 28.6 us
    all_to_all x4 -> x0, waiting for transfers between devices: 399 us -> none  [the longest x1 196 us: local(): lax.all_to_all(part_answer, 'dp', split_axis=0, concat_axis=0, tiled=True)]
    pallas_call x0 -> x1, Pallas kernels: none -> 167 us  [route(): pl.pallas_call(functools.partial(route_kernel, zn, blocks), out_shape=jax...]
    all_to_all x4 -> x0, starting transfers between devices: 44.5 us -> none  [the longest x1 18 us: local(): lax.all_to_all(wanted_rows, 'dp', split_axis=0, concat_axis=0, tiled=True)]
    unnamed x0 -> x1, blocking collectives: none -> 28.6 us
    gather x12 -> x0, local copies, waits for them, and re-layouts: 20.3 us -> none  [the longest x4 8.16 us: one_group(): jnp.take(neighbour_values, group_slots, axis=0)]
    reduce_scatter x1, waiting for transfers between devices: 41.6 us -> 61.1 us  [local(): lax.psum_scatter(jnp.dot(cross_rows, whole_weight, preferred_element_type...]
    all_to_all x1 -> x0, blocking collectives: 17.8 us -> none  [local(): lax.all_to_all(total_answer, 'dp', split_axis=0, concat_axis=0, tiled=True)]
    while x4 -> x0, other arithmetic: 16 us -> none
  transfers between devices with their start and end apart: 8 -> 4, of which waited for: 6 -> 2; matrix products, arithmetic and copies ran while one was open for 3% -> 2% of each run, Pallas kernels for 0% -> 56%
where the time goes in v1:
time: 299 us; the launch traced here: 297 us
  Pallas kernels  167 us (56%)
  waiting for transfers between devices  65 us (22%)
  blocking collectives  28.6 us (10%)
  between operations  14.9 us (5%)
  local copies, waits for them, and re-layouts  6.03 us (2%)
  starting transfers between devices  5.3 us (2%)
  other arithmetic  5.04 us (2%)
  matrix products  4.81 us (2%)
    pallas_call x1, Pallas kernels, route(): pl.pallas_call(functools.partial(route_kernel, zn, blocks), out_shape=jax...  167 us
    reduce_scatter x1, waiting for transfers between devices, local(): lax.psum_scatter(jnp.dot(cross_rows, whole_weight, preferred_element_type...  61.1 us
    unnamed x1, blocking collectives  28.6 us
  transfers between devices with their start and end apart: 4, of which 2 were waited for; matrix products, arithmetic and copies ran while one was open for 2% of the time, Pallas kernels for 56%

profile of v1, /device:TPU:1, one launch (start us, length us, event | category | flops | bytes accessed | tf_op | source)
XLA Modules:
  0.0 297.0 jit_solution(10487873603939282140)
XLA Ops:
  7.2 0.0 all-gather.2.cloned.1.call-start
  7.2 0.7 all-gather.2.cloned.1.call-update
  7.9 0.0 reduce-scatter.2.cloned.1.call-start
  7.9 0.7 slice.12
  8.6 3.9 %collective-permute-start = (bf16[1,512]{1,0:T(2,128)(2,1)S(1)}, bf16[1,512]{1,0:T(2,128)(2,1)S(1)}, u32[]{:S(2)}, u32[]{:S(2)}) collective-permute-start(bf16[1,512]{1,0:T(2,128)(2,1)S(1)} %slice.12), channel_id=1, source_target_pairs={{0,8},{8,16},{16,24},{24,32},{32,40},{40,48},{48,56},{56,64},{64,7... | collective-permute-start | bytes 3080 | tf_op jit(solution)/shard_map/ppermute | solution.py:26
  12.6 0.7 multiply_add_fusion.1
  13.3 0.1 copy.16
  13.4 0.1 reshape.251
  13.5 1.3 dynamic-slice
  15.4 0.2 dynamic-update-slice
  15.7 28.6 %all-reduce = s32[512]{0:T(512)S(1)} all-reduce(s32[512]{0:T(512)S(1)} %dynamic-update-slice), channel_id=1, replica_groups=mesh['dp'=64,'tensor'=8] {'dp'}, use_global_device_ids=true, to_apply=%add | all-reduce | flops 512 | bytes 4096
  44.3 0.1 reshape.247
  44.4 0.2 convert_reduce_fusion
  44.7 0.1 reshape.248
  44.8 0.1 dynamic-slice_reduce_fusion
  44.9 0.1 squeeze.8
  45.0 0.1 squeeze.7
  45.1 0.1 broadcast_compare_fusion
  45.2 0.3 select_reduce_fusion
  45.6 0.2 select_reduce_fusion.1
  45.8 0.1 copy.17
  45.9 0.1 reshape.246
  45.9 0.1 concatenate.9.tab
  46.0 0.0 collective-permute-done
  46.0 1.0 pad_maximum_fusion
  47.1 0.1 reshape.249
  47.2 0.0 copy-start
  47.2 1.2 copy-done
  48.4 0.0 copy-start.1
  48.4 1.2 copy-done.1
  49.6 167.3 %shard_map.113 = bf16[2,4,64,256]{3,2,1,0:T(8,128)(2,1)S(1)} custom-call(s32[328]{0:T(512)S(1)} %concatenate.9.tab, bf16[2,4,64,256]{3,2,1,0:T(8,128)(2,1)S(1)} %bitcast.10, bf16[8,128,512]{2,1,0:T(8,128)(2,1)S(1)} %copy-done, bf16[8,128,512]{2,1,0:T(8,128)(2,1)S(1)} %copy-done.1), custom_call_target="tpu_custom_call" | custom-call | flops 400000000 | bytes 16000000 | tf_op jit(solution)/shard_map/pallas_call | solution.py:385
  216.9 0.3 copy.19
  217.2 1.3 collective-permute-start.1
  218.5 0.1 slice.16
  218.6 0.0 copy-start.2
  218.6 0.0 copy-start.3
  218.6 0.0 copy-start.4
  218.6 0.0 copy-start.5
  218.7 3.2 %collective-permute-done.1 = bf16[1,512]{1,0:T(2,128)(2,1)S(1)} collective-permute-done((bf16[1,512]{1,0:T(2,128)(2,1)S(1)}, bf16[1,512]{1,0:T(2,128)(2,1)S(1)}, u32[]{:S(2)}, u32[]{:S(2)}) %collective-permute-start.1) | collective-permute-done | bytes 1056 | tf_op jit(solution)/shard_map/ppermute | solution.py:26
  221.9 0.0 all-gather.2.cloned.1.call-done
  221.9 4.8 %convolution_convert_fusion = bf16[256,4096]{1,0:T(8,128)(2,1)} fusion(bf16[512,4096]{0,1:T(8,128)(2,1)} %all-gather.2.cloned.1.call-done, bf16[1,512]{1,0:T(2,128)(2,1)S(1)} %collective-permute-done.1, bf16[255,512]{1,0:T(8,128)(2,1)S(1)} %slice.16), kind=kOutput, calls=%fused_computation | convolution fusion | flops 1075314688 | bytes 6553600 | tf_op jit(solution)/shard_map/dot_general | solution.py:439
  226.7 0.0 reduce-scatter.2.cloned.1.call-update
  226.7 61.1 %reduce-scatter.2.cloned.1.call-done = bf16[32,4096]{1,0:T(8,128)(2,1)} async-done(((bf16[256,4096]{1,0:T(8,128)(2,1)}), bf16[32,4096]{1,0:T(8,128)(2,1)}) %reduce-scatter.2.cloned.1.call-update) | async-done | bytes 262160 | tf_op jit(solution)/shard_map/reduce_scatter | solution.py:438
  287.8 0.0 copy-done.2
  287.8 0.0 copy-done.3
  287.8 1.2 fusion.24
  289.0 0.2 multiply_reduce_fusion
  289.2 0.0 copy-done.4
  289.3 0.0 copy-done.5
  289.3 0.9 add_convert_fusion
  (17 shorter events, 0.2 us)
Async XLA Ops:
  7.2 214.7 %all-gather.2.cloned.1.call-start = ((), (), s32[]{:S(2)}) async-start(), calls=%async_computation.1 | async-start | bytes 4259840 | tf_op jit(solution)/shard_map/all_gather | solution.py:437
  7.9 279.9 %reduce-scatter.2.cloned.1.call-start = ((), (), s32[]{:S(2)}) async-start(), calls=%async_computation.2 | async-start | bytes 2359296 | tf_op jit(solution)/shard_map/reduce_scatter | solution.py:438
  8.6 37.4 %collective-permute-start = (bf16[1,512]{1,0:T(2,128)(2,1)S(1)}, bf16[1,512]{1,0:T(2,128)(2,1)S(1)}, u32[]{:S(2)}, u32[]{:S(2)}) collective-permute-start(bf16[1,512]{1,0:T(2,128)(2,1)S(1)} %slice.12), channel_id=1, source_target_pairs={{0,8},{8,16},{16,24},{24,32},{32,40},{40,48},{48,56},{56,64},{64,7... | collective-permute-start | bytes 3080 | tf_op jit(solution)/shard_map/ppermute | solution.py:26
  47.2 1.2 copy-start
  48.4 1.2 copy-start.1
  217.2 4.6 %collective-permute-start.1 = (bf16[1,512]{1,0:T(2,128)(2,1)S(1)}, bf16[1,512]{1,0:T(2,128)(2,1)S(1)}, u32[]{:S(2)}, u32[]{:S(2)}) collective-permute-start(bf16[1,512]{1,0:T(2,128)(2,1)S(1)} %slice.17), channel_id=1, source_target_pairs={{8,0},{16,8},{24,16},{32,24},{40,32},{48,40},{56,48},{64,56},{72,6... | collective-permute-start | bytes 3080 | tf_op jit(solution)/shard_map/ppermute | solution.py:26
  218.6 69.2 %copy-start.2 = (s32[32,4096]{1,0:T(8,128)S(1)}, s32[32,4096]{1,0:T(8,128)}, u32[]{:S(2)}) copy-start(s32[32,4096]{1,0:T(8,128)} %param.15) | copy-start | bytes 1572868
  218.6 69.2 %copy-start.3 = (bf16[32,4096]{1,0:T(8,128)(2,1)S(1)}, bf16[32,4096]{1,0:T(8,128)(2,1)}, u32[]{:S(2)}) copy-start(bf16[32,4096]{1,0:T(8,128)(2,1)} %param.13) | copy-start | bytes 786436
  218.6 70.6 %copy-start.4 = (f32[4096]{0:T(1024)S(1)}, f32[4096]{0:T(1024)}, u32[]{:S(2)}) copy-start(f32[4096]{0:T(1024)} %param.17) | copy-start | bytes 49156
  218.6 70.6 %copy-start.5 = (f32[4096]{0:T(1024)S(1)}, f32[4096]{0:T(1024)}, u32[]{:S(2)}) copy-start(f32[4096]{0:T(1024)} %param.16) | copy-start | bytes 49156
Sparse Core Ops, SparseCore 0:
  10.9 148.1 all-gather.1
  226.8 60.9 reduce-scatter.1

commit v2 on v0

v2 whole, which is shorter than its diff:
```python
import functools

import jax
import jax.numpy as jnp
from jax import lax
from jax.experimental import pallas as pl
from jax.experimental.pallas import tpu as pltpu
from jax.sharding import PartitionSpec as P

HEAD = 128
XN = 4
GROUP = 2
NONE = -1e30

keep_rate = 0.9
norm_eps = 1e-05
MESH = pl.DeviceIdType.MESH


ORDER = (
    "k0 c g0 g1",
    "c g0 g1",
    "c g0 g1",
    "c g0 g1",
    "c g0 g1 k0 k1",
    "c g0 g1",
    "c g0 g1",
    "c g0 g1",
    "c*2 g0 g1",
    "k0 r0",
    "r0",
    "r0 k1",
    "r0",
    "k1 r0 r1",
) + ("r0 r1",) * 5 + ("r1*6",)


def shifted(x, axis, by):
    count = lax.axis_size(axis)
    pairs = [(i, i + by) for i in range(count) if 0 <= i + by < count]
    return lax.ppermute(x, axis, pairs)


def route_kernel(zn, blocks, code_ref, q_ref, k_ref, v_ref, out_ref, *scratch):
    groups = q_ref.shape[0]
    span = q_ref.shape[3] // GROUP
    wide = GROUP * HEAD
    rows = k_ref.shape[0]
    me = lax.axis_index("dp")
    tens = lax.axis_index("tensor")
    z, x = me // XN, me % XN
    z_up = ((z + 1) % zn) * XN + x
    z_dn = ((z + zn - 1) % zn) * XN + x
    x_up = z * XN + (x + 1) % XN
    x_dn = z * XN + (x + XN - 1) % XN
    per_g = 7
    bufs = [scratch[g * per_g : (g + 1) * per_g] for g in range(groups)]
    (
        codes,
        table,
        slots,
        code_send,
        code_recv,
        ag_send,
        ag_recv,
        kv_own,
        kv_send,
        kv_recv,
        rd_send,
        rd_recv,
        rs_send,
        rs_recv,
        table_sem,
    ) = scratch[groups * per_g :]
    far, near = zn // 2, zn // 2 - 1
    chains = [
        (way, b, far if (b < blocks // 2) == (way > 0) else near)
        for b in range(blocks)
        for way in (1, -1)
    ]
    started = []

    barrier = pltpu.get_barrier_semaphore()
    for peer in (z_up, z_dn, x_up, x_dn):
        pl.semaphore_signal(barrier, inc=1, device_id=(peer, tens), device_id_type=MESH)
    pl.semaphore_wait(barrier, 4)

    def copy_to(src, dst, send, recv, peer):
        return pltpu.make_async_remote_copy(
            src_ref=src,
            dst_ref=dst,
            send_sem=send,
            recv_sem=recv,
            device_id=(peer, tens),
            device_id_type=MESH,
        )

    def remote(src, dst, send, recv, peer):
        copy = copy_to(src, dst, send, recv, peer)
        copy.start()
        started.append(copy)
        return copy

    def stores(g):
        hb = rows // 2
        lo, hi = pl.ds(0, hb), pl.ds(hb, hb)
        cols = pl.ds(g * wide, wide)
        pairs = [(k_ref, bufs[g][1]), (v_ref, bufs[g][2])]
        own, first, later = [], [], []
        for n, (src, dst) in enumerate(pairs):
            whole = src.at[:, :, cols] if n == 0 else src.at[:, g]
            copy = pltpu.make_async_copy(whole, dst.at[0], kv_own.at[g, n])
            copy.start()
            own.append(copy)
        for part, place, peer, at in ((lo, 3, x_up, 0), (hi, 1, x_dn, 1), (hi, 3, x_up, 2), (lo, 1, x_dn, 3)):
            for n, (src, dst) in enumerate(pairs):
                copy = remote(
                    src.at[part, :, cols] if n == 0 else src.at[part, g],
                    dst.at[place, part],
                    kv_send.at[g, n, at],
                    kv_recv.at[g, n, at],
                    peer,
                )
                (first if at < 2 else later).append(copy)
        yield
        for i, (part, place, peer, at) in enumerate(((lo, 3, x_up, 4), (hi, 1, x_dn, 5))):
            for n, (_, dst) in enumerate(pairs):
                first[2 * i + n].wait_recv()
                later.append(
                    remote(
                        dst.at[place, part],
                        dst.at[2, part],
                        kv_send.at[g, n, at],
                        kv_recv.at[g, n, at],
                        peer,
                    )
                )
        yield
        for copy in own:
            copy.wait()
        for copy in later:
            copy.wait_recv()
        yield

    def gather_codes():
        codes[z] = code_ref[...]
        for s in range(far + 1):
            for c, (way, steps) in enumerate(((1, far), (-1, near))):
                if s > steps:
                    continue
                here = codes.at[(z - way * s + zn) % zn]
                peer = z_up if way > 0 else z_dn
                if s > 0:
                    copy_to(here, here, code_send.at[c, s - 1], code_recv.at[c, s - 1], peer).wait_recv()
                if s < steps:
                    src = code_ref if s == 0 else here
                    remote(src, here, code_send.at[c, s], code_recv.at[c, s], peer)
            yield
        copy = pltpu.make_async_copy(codes, table, table_sem)
        copy.start()
        copy.wait()

        @pl.loop(0, zn)
        def _(z0):
            asks = [table[z0, 0, k] for k in range(2 * blocks)]
            for r in range(XN):
                first = (z * XN + (x + r) % XN) * rows
                block, at = jnp.int32(0), jnp.int32(0)
                for k, ask in enumerate(asks):
                    hit = (ask >= first) & (ask < first + rows)
                    block = jnp.where(hit, k // 2, block)
                    at = jnp.where(hit, ask - first, at)
                slots[z0, r] = z0 * blocks + block
                slots[z0, XN + r] = at
            for k, ask in enumerate(asks):
                holder = ask // rows
                there = holder // XN == z
                slots[z0, 2 * XN + k] = jnp.where(there, (holder - x + XN) % XN, XN)

        yield

    def gather(g):
        col = bufs[g][0]
        for b in range(blocks):
            col[z * blocks + b] = q_ref[g, b]
        for s in range(far + 1):
            for c, (way, block, steps) in enumerate(chains):
                if s > steps:
                    continue
                here = col.at[((z - way * s + zn) % zn) * blocks + block]
                peer = z_up if way > 0 else z_dn
                if s > 0:
                    copy_to(
                        here, here, ag_send.at[g, c, s - 1], ag_recv.at[g, c, s - 1], peer
                    ).wait_recv()
                if s < steps:
                    src = q_ref.at[g, block] if s == 0 else here
                    remote(src, here, ag_send.at[g, c, s], ag_recv.at[g, c, s], peer)
            yield

    left = lax.broadcasted_iota(jnp.int32, (HEAD, GROUP * span), 1) < span
    left_bf = left.astype(jnp.float32).astype(jnp.bfloat16)
    right_bf = (1.0 - left.astype(jnp.float32)).astype(jnp.bfloat16)

    def attend(g, z0):
        col, keys, values, res, stat = bufs[g][:5]
        scale = HEAD ** (-0.5)
        for pair in range(0, XN, 2):
            places = (pair, pair + 1)
            at = [slots[z0, XN + r] for r in places]
            scores = []
            for r, a in zip(places, at):
                q = col[slots[z0, r]]
                q2 = jnp.concatenate([q * left_bf, q * right_bf], axis=0)
                scores.append(jnp.dot(keys[r, a], q2, preferred_element_type=jnp.float32))
            tops = [jnp.max(v, axis=0, keepdims=True) for v in scores]
            raised = [jnp.exp((v - t) * scale) for v, t in zip(scores, tops)]
            totals = [jnp.sum(v, axis=0, keepdims=True) for v in raised]
            for r, a, e, top, total in zip(places, at, raised, tops, totals):
                eb = e.astype(jnp.bfloat16)
                p2 = jnp.concatenate([eb * left_bf, eb * right_bf], axis=0)
                part = jnp.dot(values[r, a], p2, preferred_element_type=jnp.float32)
                res[z0 * XN + r] = (part * (1.0 / total)).astype(jnp.bfloat16)
                stat[z0, r : r + 1, :] = top * scale + jnp.log(total)
        stat[z0, XN : XN + 1, :] = jnp.full((1, GROUP * span), NONE, jnp.float32)

    def combine(g, z0, block, arrived, dst, dst_stat):
        res, stat = bufs[g][3:5]
        lses = [ref[...] for _, ref in arrived]
        vals = [ref[...] for ref, _ in arrived]
        for r in range(2):
            place = slots[z0, 2 * XN + 2 * block + r]
            lses.append(stat[z0, pl.ds(place, 1), :])
            vals.append(res[z0 * XN + jnp.minimum(place, XN - 1)])
        top = functools.reduce(jnp.maximum, lses)
        weights = [jnp.exp(v - top) for v in lses]
        total = functools.reduce(jnp.add, weights)
        if dst_stat is not None:
            dst_stat[...] = top + jnp.log(total)
        share = 1.0 / total
        acc = vals[0].astype(jnp.float32) * (weights[0] * share)
        for v, w in zip(vals[1:], weights[1:]):
            acc += v.astype(jnp.float32) * (w * share)
        dst[...] = acc.astype(jnp.bfloat16)

    def reduce(g):
        ring, ring_stat = bufs[g][5:7]
        attend(g, (z + far) % zn)
        for s in range(far + 1):
            for c, (way, block, steps) in enumerate(chains):
                i = s - (far - steps)
                if i < 0 or i > steps:
                    continue
                here, here_stat = ring.at[c, i], ring_stat.at[c, i, pl.ds(0, 1)]
                peer = z_up if way > 0 else z_dn
                if i > 0:
                    for ref, snd, rcv in (
                        (here, rd_send, rd_recv),
                        (here_stat, rs_send, rs_recv),
                    ):
                        copy_to(
                            ref, ref, snd.at[g, c, i - 1], rcv.at[g, c, i - 1], peer
                        ).wait_recv()
                if i < steps:
                    z0 = (z + way * (steps - i) + zn) % zn
                    arrived = [(here, here_stat)] if i > 0 else []
                    combine(g, z0, block, arrived, here, here_stat)
                    remote(
                        here_stat,
                        ring_stat.at[c, i + 1, pl.ds(0, 1)],
                        rs_send.at[g, c, i],
                        rs_recv.at[g, c, i],
                        peer,
                    )
                    remote(
                        here,
                        ring.at[c, i + 1],
                        rd_send.at[g, c, i],
                        rd_recv.at[g, c, i],
                        peer,
                    )
            away = far - (s + 1)
            if away > 0:

                @pl.loop(0, 2)
                def _(n):
                    attend(g, (z + (1 - 2 * n) * away + zn) % zn)

            elif away == 0:
                attend(g, z)
            yield
        for b in range(blocks):
            arrived = [
                (ring.at[c, steps], ring_stat.at[c, steps, pl.ds(0, 1)])
                for c, (_, block, steps) in enumerate(chains)
                if block == b
            ]
            combine(g, z, b, arrived, out_ref.at[g, b], None)
        yield

    live = {"c": gather_codes()}
    parts = {"g": gather, "k": stores, "r": reduce}
    for step in ORDER:
        for token in step.split():
            name, times = token.split("*") if "*" in token else (token, "1")
            if name not in live:
                live[name] = parts[name[0]](int(name[1:]))
            for _ in range(int(times)):
                next(live[name], None)
    for it in live.values():
        for _ in it:
            pass
    for copy in started:
        copy.wait_send()


def route(code, q, k, v):
    groups, blocks, deep, wide = q.shape
    rows = k.shape[0]
    zn = lax.axis_size("dp") // XN
    steps = zn // 2
    bf, f32 = jnp.bfloat16, jnp.float32
    per_group = [
        pltpu.VMEM((zn * blocks, deep, wide), bf),
        pltpu.VMEM((XN, rows, k.shape[1], GROUP * HEAD), bf),
        pltpu.VMEM((XN, rows) + v.shape[2:], bf),
        pltpu.VMEM((zn * XN, deep, wide), bf),
        pltpu.VMEM((zn, 8, wide), f32),
        pltpu.VMEM((2 * blocks, steps + 1, deep, wide), bf),
        pltpu.VMEM((2 * blocks, steps + 1, 8, wide), f32),
    ]
    dma = pltpu.SemaphoreType.DMA
    vmem = pl.BlockSpec(memory_space=pltpu.VMEM)
    hbm = pl.BlockSpec(memory_space=pl.ANY)
    ring = dma((groups, 2 * blocks, steps))
    return pl.pallas_call(
        functools.partial(route_kernel, zn, blocks),
        out_shape=jax.ShapeDtypeStruct(q.shape, bf),
        in_specs=[vmem, vmem, hbm, hbm],
        out_specs=vmem,
        scratch_shapes=per_group * groups
        + [
            pltpu.VMEM((zn, 8, HEAD), jnp.int32),
            pltpu.SMEM((zn, 8, HEAD), jnp.int32),
            pltpu.SMEM((zn, 2 * XN + 2 * blocks), jnp.int32),
            dma((2, steps)),
            dma((2, steps)),
            ring,
            ring,
            dma((groups, 2)),
            dma((groups, 2, 6)),
            dma((groups, 2, 6)),
            ring,
            ring,
            ring,
            ring,
            dma,
        ],
        compiler_params=pltpu.CompilerParams(
            collective_id=0, has_side_effects=True, vmem_limit_bytes=56 * 1024 * 1024
        ),
        cost_estimate=pl.CostEstimate(
            flops=1_100_000_000, bytes_accessed=16_000_000, transcendentals=2_200_000
        ),
    )(code, q, k, v)


def local(
    queries,
    neighbour_keys,
    neighbour_values,
    residual,
    out_weight,
    drop_mask,
    norm_gain,
    norm_bias,
    neighbour_owner,
    neighbour_slot,
):
    row_width = queries.shape[1]
    blocks = neighbour_owner.shape[0]
    span = queries.shape[0] // blocks
    groups = row_width // (GROUP * HEAD)
    code = (neighbour_owner * neighbour_keys.shape[0] + neighbour_slot).reshape(1, -1)
    code = jnp.pad(code, ((0, 7), (0, HEAD - code.shape[1])))
    carried = shifted(queries[-1:], "dp", 1)
    asked = jnp.concatenate([carried, queries[:-1]], axis=0)
    asked = asked.reshape(blocks, span, groups, GROUP, HEAD).transpose(2, 0, 4, 3, 1)
    asked = asked.reshape(groups, blocks, HEAD, GROUP * span)
    rows, length, _ = neighbour_values.shape
    values = neighbour_values.reshape(rows, length, groups, GROUP, HEAD).transpose(0, 2, 4, 3, 1)
    values = values.reshape(rows, groups, HEAD, GROUP * length)
    merged = route(code, asked, neighbour_keys, values)
    merged = merged.reshape(groups, blocks, HEAD, GROUP, span).transpose(1, 4, 0, 3, 2)
    flat_rows = merged.reshape(-1, row_width)
    following = shifted(flat_rows[:1], "dp", -1)
    cross_rows = jnp.concatenate([flat_rows[1:], following], axis=0)
    whole_weight = lax.all_gather(out_weight, "dp", axis=1, tiled=True)
    branch = lax.psum_scatter(
        jnp.dot(cross_rows, whole_weight, preferred_element_type=jnp.float32).astype(jnp.bfloat16),
        "tensor",
        scatter_dimension=0,
        tiled=True,
    ).astype(jnp.float32)
    keep_scale = drop_mask.astype(jnp.float32) * (1.0 / keep_rate)
    stream = residual.astype(jnp.float32) + keep_scale * branch
    centre = jnp.mean(stream, axis=1, keepdims=True)
    spread = jnp.mean(jnp.square(stream - centre), axis=1, keepdims=True)
    normed = (stream - centre) * lax.rsqrt(spread + norm_eps) * norm_gain + norm_bias
    return (stream.astype(jnp.bfloat16), normed.astype(jnp.bfloat16))


def solution(mesh):
    placed = (
        P("dp", "tensor"),
        P("dp", None, "tensor"),
        P("dp", None, "tensor"),
        P(("dp", "tensor"), None),
        P("tensor", "dp"),
        P(("dp", "tensor"), None),
        P(),
        P(),
        P("dp", None),
        P("dp", None),
    )
    return jax.shard_map(
        local,
        mesh=mesh,
        in_specs=placed,
        out_specs=(P(("dp", "tensor"), None), P(("dp", "tensor"), None)),
        check_vma=False,
    )
```

time: 647 us -> 228 us (0.35)
  waiting for transfers between devices: 450 us -> 52.2 us
  Pallas kernels: 0 us -> 138 us
  local copies, waits for them, and re-layouts: 64.1 us -> 9.18 us
  starting transfers between devices: 49.8 us -> 5.3 us
  other arithmetic: 28.7 us -> 3.14 us
  blocking collectives: 17.8 us -> 0 us
  matrix products: 20.2 us -> 4.79 us
    all_to_all x4 -> x0, waiting for transfers between devices: 399 us -> none  [the longest x1 196 us: local(): lax.all_to_all(part_answer, 'dp', split_axis=0, concat_axis=0, tiled=True)]
    pallas_call x0 -> x1, Pallas kernels: none -> 138 us  [route(): pl.pallas_call(functools.partial(route_kernel, zn, blocks), out_shape=jax...]
    all_to_all x4 -> x0, starting transfers between devices: 44.5 us -> none  [the longest x1 18 us: local(): lax.all_to_all(wanted_rows, 'dp', split_axis=0, concat_axis=0, tiled=True)]
    gather x12 -> x0, local copies, waits for them, and re-layouts: 20.3 us -> none  [the longest x4 8.16 us: one_group(): jnp.take(neighbour_values, group_slots, axis=0)]
    all_to_all x1 -> x0, blocking collectives: 17.8 us -> none  [local(): lax.all_to_all(total_answer, 'dp', split_axis=0, concat_axis=0, tiled=True)]
    while x4 -> x0, other arithmetic: 16 us -> none
    dot_general x9 -> x0, matrix products: 15.4 us -> none  [the longest x4 7.44 us: attend_block(): jnp.einsum('bhrl,blhe->brhe', weights, value_heads, preferred_element_typ...]
    convert_element_type x5 -> x0, local copies, waits for them, and re-layouts: 11.8 us -> none  [the longest x4 7.39 us: attend_block(): partial_value.astype(jnp.bfloat16).reshape(count_b, count_r, row_width)]
  transfers between devices with their start and end apart: 8 -> 4, of which waited for: 6 -> 2; matrix products, arithmetic and copies ran while one was open for 3% -> 4% of each run, Pallas kernels for 0% -> 61%
where the time goes in v2:
time: 228 us; the launch traced here: 227 us
  Pallas kernels  138 us (61%)
  waiting for transfers between devices  52.2 us (23%)
  between operations  14.2 us (6%)
  local copies, waits for them, and re-layouts  9.18 us (4%)
  starting transfers between devices  5.3 us (2%)
  matrix products  4.79 us (2%)
  other arithmetic  3.14 us (1%)
    pallas_call x1, Pallas kernels, route(): pl.pallas_call(functools.partial(route_kernel, zn, blocks), out_shape=jax...  138 us
    reduce_scatter x1, waiting for transfers between devices, local(): lax.psum_scatter(jnp.dot(cross_rows, whole_weight, preferred_element_type...  48.2 us
    ppermute x2, starting transfers between devices, shifted(): return lax.ppermute(x, axis, pairs)  5.22 us
    dot_general x1, matrix products, local(): jnp.dot(cross_rows, whole_weight, preferred_element_type=jnp.float32)  4.79 us
  transfers between devices with their start and end apart: 4, of which 2 were waited for; matrix products, arithmetic and copies ran while one was open for 4% of the time, Pallas kernels for 61%

profile of v2, /device:TPU:1, one launch (start us, length us, event | category | flops | bytes accessed | tf_op | source)
XLA Modules:
  0.0 226.7 jit_solution(16503626075074998910)
XLA Ops:
  7.2 0.0 copy-start.1
  7.2 0.0 all-gather.2.cloned.1.call-start
  7.2 0.7 all-gather.2.cloned.1.call-update
  7.9 0.0 reduce-scatter.2.cloned.1.call-start
  8.0 0.7 slice.12
  8.7 3.9 %collective-permute-start = (bf16[1,512]{1,0:T(2,128)(2,1)S(1)}, bf16[1,512]{1,0:T(2,128)(2,1)S(1)}, u32[]{:S(2)}, u32[]{:S(2)}) collective-permute-start(bf16[1,512]{1,0:T(2,128)(2,1)S(1)} %slice.12), channel_id=1, source_target_pairs={{0,8},{8,16},{16,24},{24,32},{32,40},{40,48},{48,56},{56,64},{64,7... | collective-permute-start | bytes 3080 | tf_op jit(solution)/shard_map/ppermute | solution.py:41
  12.6 0.7 multiply_add_fusion.1
  13.3 1.3 reshape.42
  14.6 2.3 %copy.22 = bf16[8,128,2,2,128]{1,3,4,2,0:T(2,128)(2,1)S(1)} copy(bf16[8,128,2,2,128]{4,3,2,1,0:T(2,128)(2,1)S(1)} %reshape.42) | data formatting | bytes 2097152 | tf_op jit(solution)/shard_map/reshape | solution.py:391
  17.0 1.5 reshape.43.v_ref
  18.5 0.1 copy.20
  18.5 0.1 reshape.39
  18.6 0.6 pad.4.code_ref
  19.2 0.0 collective-permute-done
  19.2 0.0 copy-done.1
  19.2 0.1 pad_maximum_fusion
  19.3 0.1 reshape.40
  19.4 0.9 copy.23.q_ref
  20.3 137.9 %shard_map.113 = bf16[2,4,128,128]{3,2,1,0:T(8,128)(2,1)} custom-call(s32[8,128]{1,0:T(8,128)} %pad.4.code_ref, bf16[2,4,128,128]{3,2,1,0:T(8,128)(2,1)} %copy.23.q_ref, bf16[8,128,512]{2,1,0:T(8,128)(2,1)} %k_ref.1, bf16[8,2,128,256]{3,2,1,0:T(8,128)(2,1)} %reshape.43.v_ref), custom_call_target="tpu_custom_call" | custom-call | flops 1100000000 | bytes 16000000 | tf_op jit(solution)/shard_map/pallas_call | solution.py:336
  158.2 1.1 copy.24
  159.3 0.3 copy.25
  159.6 0.1 reshape.45
  159.7 1.3 collective-permute-start.1
  161.0 0.1 slice.16
  161.1 0.0 copy-start
  161.1 0.0 copy-start.2
  161.1 0.0 copy-start.3
  161.2 0.0 copy-start.4
  161.2 3.3 %collective-permute-done.1 = bf16[1,512]{1,0:T(2,128)(2,1)S(1)} collective-permute-done((bf16[1,512]{1,0:T(2,128)(2,1)S(1)}, bf16[1,512]{1,0:T(2,128)(2,1)S(1)}, u32[]{:S(2)}, u32[]{:S(2)}) %collective-permute-start.1) | collective-permute-done | bytes 1056 | tf_op jit(solution)/shard_map/ppermute | solution.py:41
  164.5 0.0 all-gather.2.cloned.1.call-done
  164.5 4.8 %convolution_convert_fusion = bf16[256,4096]{1,0:T(8,128)(2,1)} fusion(bf16[512,4096]{0,1:T(8,128)(2,1)} %all-gather.2.cloned.1.call-done, bf16[1,512]{1,0:T(2,128)(2,1)S(1)} %collective-permute-done.1, bf16[255,512]{1,0:T(8,128)(2,1)S(1)} %slice.16), kind=kOutput, calls=%fused_computation | convolution fusion | flops 1075314688 | bytes 6553600 | tf_op jit(solution)/shard_map/dot_general | solution.py:400
  169.3 0.0 reduce-scatter.2.cloned.1.call-update
  169.3 48.2 %reduce-scatter.2.cloned.1.call-done = bf16[32,4096]{1,0:T(8,128)(2,1)} async-done(((bf16[256,4096]{1,0:T(8,128)(2,1)}), bf16[32,4096]{1,0:T(8,128)(2,1)}) %reduce-scatter.2.cloned.1.call-update) | async-done | bytes 262160 | tf_op jit(solution)/shard_map/reduce_scatter | solution.py:399
  217.5 0.0 copy-done
  217.5 0.0 copy-done.2
  217.5 1.2 fusion.4
  218.7 0.2 multiply_reduce_fusion
  218.9 0.0 copy-done.3
  218.9 0.0 copy-done.4
  218.9 0.9 add_convert_fusion
  (4 shorter events, 0.1 us)
Async XLA Ops:
  7.2 12.1 %copy-start.1 = (bf16[256,512]{1,0:T(8,128)(2,1)S(1)}, bf16[256,512]{1,0:T(8,128)(2,1)}, u32[]{:S(2)}) copy-start(bf16[256,512]{1,0:T(8,128)(2,1)} %param.10) | copy-start | bytes 786436
  7.2 157.3 %all-gather.2.cloned.1.call-start = ((), (), s32[]{:S(2)}) async-start(), calls=%async_computation.1 | async-start | bytes 4259840 | tf_op jit(solution)/shard_map/all_gather | solution.py:398
  7.9 209.6 %reduce-scatter.2.cloned.1.call-start = ((), (), s32[]{:S(2)}) async-start(), calls=%async_computation.2 | async-start | bytes 2359296 | tf_op jit(solution)/shard_map/reduce_scatter | solution.py:399
  8.7 10.6 %collective-permute-start = (bf16[1,512]{1,0:T(2,128)(2,1)S(1)}, bf16[1,512]{1,0:T(2,128)(2,1)S(1)}, u32[]{:S(2)}, u32[]{:S(2)}) collective-permute-start(bf16[1,512]{1,0:T(2,128)(2,1)S(1)} %slice.12), channel_id=1, source_target_pairs={{0,8},{8,16},{16,24},{24,32},{32,40},{40,48},{48,56},{56,64},{64,7... | collective-permute-start | bytes 3080 | tf_op jit(solution)/shard_map/ppermute | solution.py:41
  159.7 4.7 %collective-permute-start.1 = (bf16[1,512]{1,0:T(2,128)(2,1)S(1)}, bf16[1,512]{1,0:T(2,128)(2,1)S(1)}, u32[]{:S(2)}, u32[]{:S(2)}) collective-permute-start(bf16[1,512]{1,0:T(2,128)(2,1)S(1)} %slice.17), channel_id=1, source_target_pairs={{8,0},{16,8},{24,16},{32,24},{40,32},{48,40},{56,48},{64,56},{72,6... | collective-permute-start | bytes 3080 | tf_op jit(solution)/shard_map/ppermute | solution.py:41
  161.1 56.3 %copy-start = (s32[32,4096]{1,0:T(8,128)S(1)}, s32[32,4096]{1,0:T(8,128)}, u32[]{:S(2)}) copy-start(s32[32,4096]{1,0:T(8,128)} %param.15) | copy-start | bytes 1572868
  161.1 56.3 %copy-start.2 = (bf16[32,4096]{1,0:T(8,128)(2,1)S(1)}, bf16[32,4096]{1,0:T(8,128)(2,1)}, u32[]{:S(2)}) copy-start(bf16[32,4096]{1,0:T(8,128)(2,1)} %param.13) | copy-start | bytes 786436
  161.1 57.8 %copy-start.3 = (f32[4096]{0:T(1024)S(1)}, f32[4096]{0:T(1024)}, u32[]{:S(2)}) copy-start(f32[4096]{0:T(1024)} %param.17) | copy-start | bytes 49156
  161.2 57.8 %copy-start.4 = (f32[4096]{0:T(1024)S(1)}, f32[4096]{0:T(1024)}, u32[]{:S(2)}) copy-start(f32[4096]{0:T(1024)} %param.16) | copy-start | bytes 49156
Sparse Core Ops, SparseCore 0:
  11.0 149.8 all-gather.1
  169.4 47.9 reduce-scatter.1

commit v3 on v2

--- a/solution.py
+++ b/solution.py
@@ -18,21 +18,18 @@
 
 
 ORDER = (
-    "k0 c g0 g1",
-    "c g0 g1",
-    "c g0 g1",
-    "c g0 g1",
-    "c g0 g1 k0 k1",
-    "c g0 g1",
-    "c g0 g1",
-    "c g0 g1",
-    "c*2 g0 g1",
-    "k0 r0",
-    "r0",
-    "r0 k1",
-    "r0",
-    "k1 r0 r1",
-) + ("r0 r1",) * 5 + ("r1*6",)
+    [("k0", "c", "g0", "g1")]
+    + [("c", "g0", "g1")] * 3
+    + [("c", "g0", "g1", "k0", "k1")]
+    + [("w", "c", "g0", "g1")] * 3
+    + [("w", "c", "c", "g0", "g1"), ("k0",)]
+    + [("w", "r0")] * 3
+    + [("k1", "w", "r0"), ("w", "r0"), ("k1", "w", "r0", "r1")]
+    + [("r0", "r1")] * 2
+    + [("w", "r0", "r1"), ("r0", "r1"), ("r1",), ("w",), ("r1",)]
+)
+YN = 4
+CUTS = 4
 
 
 def shifted(x, axis, by):
@@ -41,7 +38,22 @@
     return lax.ppermute(x, axis, pairs)
 
 
-def route_kernel(zn, blocks, code_ref, q_ref, k_ref, v_ref, out_ref, *scratch):
+def layer_kernel(
+    zn,
+    blocks,
+    code_ref,
+    q_ref,
+    k_ref,
+    v_ref,
+    w_ref,
+    residual_ref,
+    drop_ref,
+    gain_ref,
+    bias_ref,
+    next_ref,
+    normed_ref,
+    *scratch,
+):
     groups = q_ref.shape[0]
     span = q_ref.shape[3] // GROUP
     wide = GROUP * HEAD
@@ -53,6 +65,13 @@
     z_dn = ((z + zn - 1) % zn) * XN + x
     x_up = z * XN + (x + 1) % XN
     x_dn = z * XN + (x + XN - 1) % XN
+    devices = zn * XN
+    d_next = (me + 1) % devices
+    d_prev = (me + devices - 1) % devices
+    y, core = tens // 2, tens % 2
+    y_up = ((y + 1) % YN) * 2 + core
+    y_dn = ((y + YN - 1) % YN) * 2 + core
+    partner = y * 2 + 1 - core
     per_g = 7
     bufs = [scratch[g * per_g : (g + 1) * per_g] for g in range(groups)]
     (
@@ -71,6 +90,26 @@
         rs_send,
         rs_recv,
         table_sem,
+        weight,
+        merged,
+        rows_f32,
+        sums,
+        a_out,
+        a_in,
+        far_out,
+        far_in,
+        near_out,
+        near_in,
+        w_send,
+        w_recv,
+        wx_send,
+        wx_recv,
+        h_send,
+        h_recv,
+        a_send,
+        a_recv,
+        b_send,
+        b_recv,
     ) = scratch[groups * per_g :]
     far, near = zn // 2, zn // 2 - 1
     chains = [
@@ -81,9 +120,11 @@
     started = []
 
     barrier = pltpu.get_barrier_semaphore()
-    for peer in (z_up, z_dn, x_up, x_dn):
+    for peer in (z_up, z_dn, x_up, x_dn, d_next, d_prev):
         pl.semaphore_signal(barrier, inc=1, device_id=(peer, tens), device_id_type=MESH)
-    pl.semaphore_wait(barrier, 4)
+    for peer in (y_up, y_dn, partner):
+        pl.semaphore_signal(barrier, inc=1, device_id=(me, peer), device_id_type=MESH)
+    pl.semaphore_wait(barrier, 9)
 
     def copy_to(src, dst, send, recv, peer):
         return pltpu.make_async_remote_copy(
@@ -91,7 +132,7 @@
             dst_ref=dst,
             send_sem=send,
             recv_sem=recv,
-            device_id=(peer, tens),
+            device_id=peer if isinstance(peer, tuple) else (peer, tens),
             device_id_type=MESH,
         )
 
@@ -295,31 +336,185 @@
                 for c, (_, block, steps) in enumerate(chains)
                 if block == b
             ]
-            combine(g, z, b, arrived, out_ref.at[g, b], None)
-        yield
-
-    live = {"c": gather_codes()}
+            combine(g, z, b, arrived, merged.at[g, b], None)
+            turned = jnp.transpose(merged[g, b].astype(jnp.float32))
+            for h in range(GROUP):
+                at = (g * GROUP + h) * HEAD
+                rows_f32[b * span : (b + 1) * span, at : at + HEAD] = turned[
+                    h * span : (h + 1) * span
+                ]
+        cols = pl.ds(g * wide, wide)
+        halo.append(
+            remote(
+                rows_f32.at[pl.ds(0, 8), cols],
+                rows_f32.at[pl.ds(blocks * span, 8), cols],
+                h_send.at[g],
+                h_recv.at[g],
+                d_prev,
+            )
+        )
+        yield
+
+    def gather_weight():
+        weight[z, x] = w_ref[...]
+        for s in range(far + 1):
+            for c, (way, steps) in enumerate(((1, far), (-1, near))):
+                if s > steps:
+                    continue
+                here = weight.at[(z - way * s + zn) % zn, x]
+                peer = z_up if way > 0 else z_dn
+                if s > 0:
+                    copy_to(here, here, w_send.at[c, s - 1], w_recv.at[c, s - 1], peer).wait_recv()
+                if s < steps:
+                    src = w_ref if s == 0 else here
+                    remote(src, here, w_send.at[c, s], w_recv.at[c, s], peer)
+            yield
+        lo, hi = pl.ds(0, zn // 2), pl.ds(zn // 2, zn // 2)
+
+        def send(part, column, peer, at):
+            here = weight.at[part, column]
+            return remote(here, here, wx_send.at[at], wx_recv.at[at], peer)
+
+        first = [send(lo, x, x_up, 0), send(hi, x, x_dn, 1)]
+        later = [send(hi, x, x_up, 2), send(lo, x, x_dn, 3)]
+        yield
+        first[0].wait_recv()
+        later.append(send(lo, (x + XN - 1) % XN, x_up, 4))
+        first[1].wait_recv()
+        later.append(send(hi, (x + 1) % XN, x_dn, 5))
+        yield
+        for copy in later:
+            copy.wait_recv()
+        yield
+
+    def project():
+        total = blocks * span
+        width = next_ref.shape[1]
+        depth = rows_f32.shape[1]
+        own = total // (2 * YN)
+        cut = width // CUTS
+        zs = zn // CUTS
+        half = own // 2
+        up, dn, op = (y + 1) % YN, (y + YN - 1) % YN, (y + 2) % YN
+        lo, hi = pl.ds(0, half), pl.ds(half, half)
+        for copy in halo:
+            copy.wait_recv()
+        cross = rows_f32[1 : total + 1, :]
+        ends = lax.broadcasted_iota(jnp.int32, (total, depth), 0) == total - 1
+        cross = jnp.where(ends & (me == devices - 1), 0.0, cross).astype(jnp.bfloat16)
+        a_copy, opposite, lone, shared = [], [], [], []
+        for n in range(CUTS):
+            for i in range(zs):
+                part = weight[n * zs + i].reshape(width // zn, depth)
+                product = lax.dot_general(
+                    cross, part, (((1,), (1,)), ((), ())), preferred_element_type=jnp.float32
+                )
+                at = n * cut + i * (width // zn)
+                sums[:, :, at : at + width // zn] = product.reshape(2 * YN, own, width // zn)
+            cols = slice(n * cut, (n + 1) * cut)
+            for other in range(YN):
+                a_out[n, other] = sums[other * 2 + 1 - core, :, cols].astype(jnp.bfloat16)
+            a_copy.append(
+                remote(a_out.at[n], a_in.at[n], a_send.at[n], a_recv.at[n], (me, partner))
+            )
+
+        def send(src, dst, n, at, peer):
+            return remote(src, dst, b_send.at[n, at], b_recv.at[n, at], (me, peer))
+
+        def chip_sum(n):
+            cols = slice(n * cut, (n + 1) * cut)
+            a_copy[n].wait_recv()
+            for other in range(YN):
+                sums[other * 2 + core, :, cols] += a_in[n, other].astype(jnp.float32)
+            far_out[n] = sums[op * 2 + core, :, cols].astype(jnp.bfloat16)
+            opposite.append(
+                (
+                    send(far_out.at[n, lo], far_in.at[n, lo], n, 0, y_up),
+                    send(far_out.at[n, hi], far_in.at[n, hi], n, 1, y_dn),
+                )
+            )
+            near_out[n, 0, half:, :] = sums[up * 2 + core, half:, cols].astype(jnp.bfloat16)
+            near_out[n, 1, :half, :] = sums[dn * 2 + core, :half, cols].astype(jnp.bfloat16)
+            lone.append(
+                (
+                    send(near_out.at[n, 0, hi], near_in.at[n, 0, hi], n, 2, y_up),
+                    send(near_out.at[n, 1, lo], near_in.at[n, 1, lo], n, 3, y_dn),
+                )
+            )
+
+        def pass_on(n):
+            cols = slice(n * cut, (n + 1) * cut)
+            for copy in opposite[n]:
+                copy.wait_recv()
+            mine = sums[up * 2 + core, :half, cols] + far_in[n, :half, :].astype(jnp.float32)
+            near_out[n, 0, :half, :] = mine.astype(jnp.bfloat16)
+            mine = sums[dn * 2 + core, half:, cols] + far_in[n, half:, :].astype(jnp.float32)
+            near_out[n, 1, half:, :] = mine.astype(jnp.bfloat16)
+            shared.append(
+                (
+                    send(near_out.at[n, 0, lo], near_in.at[n, 0, lo], n, 4, y_up),
+                    send(near_out.at[n, 1, hi], near_in.at[n, 1, hi], n, 5, y_dn),
+                )
+            )
+
+        def stream(n):
+            cols = slice(n * cut, (n + 1) * cut)
+            for copy in lone[n] + shared[n]:
+                copy.wait_recv()
+            branch = sums[tens, :, cols]
+            for side in range(2):
+                branch += near_in[n, side].astype(jnp.float32)
+            keep = drop_ref[:, cols].astype(jnp.float32) * (1.0 / keep_rate)
+            value = residual_ref[:, cols].astype(jnp.float32) + keep * branch
+            sums[tens, :, cols] = value
+            next_ref[:, cols] = value.astype(jnp.bfloat16)
+            return jnp.sum(value, axis=1, keepdims=True)
+
+        tally = jnp.zeros((own, 1), jnp.float32)
+        for n in range(CUTS + 2):
+            if n < CUTS:
+                chip_sum(n)
+            if 1 <= n <= CUTS:
+                pass_on(n - 1)
+            if n >= 2:
+                tally += stream(n - 2)
+        centre = tally / width
+        spread = jnp.zeros((own, 1), jnp.float32)
+        for at in range(0, width, cut):
+            off = sums[tens, :, at : at + cut] - centre
+            spread += jnp.sum(off * off, axis=1, keepdims=True)
+        scale = lax.rsqrt(spread / width + norm_eps)
+        for at in range(0, width, cut):
+            cols = slice(at, at + cut)
+            normed = (sums[tens, :, cols] - centre) * scale * gain_ref[:, cols] + bias_ref[:, cols]
+            normed_ref[:, cols] = normed.astype(jnp.bfloat16)
+
+    halo = []
+    live = {"c": gather_codes(), "w": gather_weight()}
     parts = {"g": gather, "k": stores, "r": reduce}
     for step in ORDER:
-        for token in step.split():
-            name, times = token.split("*") if "*" in token else (token, "1")
+        for name in step:
             if name not in live:
                 live[name] = parts[name[0]](int(name[1:]))
-            for _ in range(int(times)):
-                next(live[name], None)
+            next(live[name], None)
     for it in live.values():
         for _ in it:
             pass
+    project()
     for copy in started:
         copy.wait_send()
 
 
-def route(code, q, k, v):
+def layer(code, q, k, v, weight, residual, drop, gain, bias):
     groups, blocks, deep, wide = q.shape
     rows = k.shape[0]
     zn = lax.axis_size("dp") // XN
     steps = zn // 2
     bf, f32 = jnp.bfloat16, jnp.float32
+    own, width = residual.shape
+    depth = weight.shape[1]
+    cut = width // CUTS
+    span = wide // GROUP
     per_group = [
         pltpu.VMEM((zn * blocks, deep, wide), bf),
         pltpu.VMEM((XN, rows, k.shape[1], GROUP * HEAD), bf),
@@ -334,10 +529,10 @@
     hbm = pl.BlockSpec(memory_space=pl.ANY)
     ring = dma((groups, 2 * blocks, steps))
     return pl.pallas_call(
-        functools.partial(route_kernel, zn, blocks),
-        out_shape=jax.ShapeDtypeStruct(q.shape, bf),
-        in_specs=[vmem, vmem, hbm, hbm],
-        out_specs=vmem,
+        functools.partial(layer_kernel, zn, blocks),
+        out_shape=[jax.ShapeDtypeStruct(residual.shape, bf)] * 2,
+        in_specs=[vmem, vmem, hbm, hbm] + [vmem] * 5,
+        out_specs=[vmem, vmem],
         scratch_shapes=per_group * groups
         + [
             pltpu.VMEM((zn, 8, HEAD), jnp.int32),
@@ -355,14 +550,34 @@
             ring,
             ring,
             dma,
+            pltpu.VMEM((zn, XN) + weight.shape, bf),
+            pltpu.VMEM((groups, blocks, deep, wide), bf),
+            pltpu.VMEM((blocks * span + 8, depth), f32),
+            pltpu.VMEM((2 * YN, own, width), f32),
+            pltpu.VMEM((CUTS, YN, own, cut), bf),
+            pltpu.VMEM((CUTS, YN, own, cut), bf),
+            pltpu.VMEM((CUTS, own, cut), bf),
+            pltpu.VMEM((CUTS, own, cut), bf),
+            pltpu.VMEM((CUTS, 2, own, cut), bf),
+            pltpu.VMEM((CUTS, 2, own, cut), bf),
+            dma((2, steps)),
+            dma((2, steps)),
+            dma((6,)),
+            dma((6,)),
+            dma((groups,)),
+            dma((groups,)),
+            dma((CUTS,)),
+            dma((CUTS,)),
+            dma((CUTS, 6)),
+            dma((CUTS, 6)),
         ],
         compiler_params=pltpu.CompilerParams(
             collective_id=0, has_side_effects=True, vmem_limit_bytes=56 * 1024 * 1024
         ),
         cost_estimate=pl.CostEstimate(
-            flops=1_100_000_000, bytes_accessed=16_000_000, transcendentals=2_200_000
+            flops=2_200_000_000, bytes_accessed=6_000_000, transcendentals=2_200_000
         ),
-    )(code, q, k, v)
+    )(code, q, k, v, weight, residual, drop, gain, bias)
 
 
 def local(
@@ -390,24 +605,19 @@
     rows, length, _ = neighbour_values.shape
     values = neighbour_values.reshape(rows, length, groups, GROUP, HEAD).transpose(0, 2, 4, 3, 1)
     values = values.reshape(rows, groups, HEAD, GROUP * length)
-    merged = route(code, asked, neighbour_keys, values)
-    merged = merged.reshape(groups, blocks, HEAD, GROUP, span).transpose(1, 4, 0, 3, 2)
-    flat_rows = merged.reshape(-1, row_width)
-    following = shifted(flat_rows[:1], "dp", -1)
-    cross_rows = jnp.concatenate([flat_rows[1:], following], axis=0)
-    whole_weight = lax.all_gather(out_weight, "dp", axis=1, tiled=True)
-    branch = lax.psum_scatter(
-        jnp.dot(cross_rows, whole_weight, preferred_element_type=jnp.float32).astype(jnp.bfloat16),
-        "tensor",
-        scatter_dimension=0,
-        tiled=True,
-    ).astype(jnp.float32)
-    keep_scale = drop_mask.astype(jnp.float32) * (1.0 / keep_rate)
-    stream = residual.astype(jnp.float32) + keep_scale * branch
-    centre = jnp.mean(stream, axis=1, keepdims=True)
-    spread = jnp.mean(jnp.square(stream - centre), axis=1, keepdims=True)
-    normed = (stream - centre) * lax.rsqrt(spread + norm_eps) * norm_gain + norm_bias
-    return (stream.astype(jnp.bfloat16), normed.astype(jnp.bfloat16))
+    return tuple(
+        layer(
+            code,
+            asked,
+            neighbour_keys,
+            values,
+            out_weight.T,
+            residual,
+            drop_mask,
+            norm_gain.reshape(1, -1),
+            norm_bias.reshape(1, -1),
+        )
+    )
 
 
 def solution(mesh):

time: 228 us -> 172 us (0.75)
  waiting for transfers between devices: 52.2 us -> 0.01 us
  Pallas kernels: 138 us -> 156 us
  between operations: 14.2 us -> 0.74 us
  matrix products: 4.79 us -> 0 us
  other arithmetic: 3.14 us -> 0.07 us
    reduce_scatter x1 -> x0, waiting for transfers between devices: 48.2 us -> none  [local(): lax.psum_scatter(jnp.dot(cross_rows, whole_weight, preferred_element_type...]
    pallas_call x1, Pallas kernels: 138 us -> 156 us  [layer(): pl.pallas_call(functools.partial(layer_kernel, zn, blocks), out_shape=[ja...]
    dot_general x1 -> x0, matrix products: 4.79 us -> none  [local(): jnp.dot(cross_rows, whole_weight, preferred_element_type=jnp.float32)]
    ppermute x2 -> x1, waiting for transfers between devices: 3.31 us -> 0.01 us  [shifted(): return lax.ppermute(x, axis, pairs)]
    unnamed x10, local copies, waits for them, and re-layouts: 0.03 us -> 2.43 us
    ppermute x2 -> x1, starting transfers between devices: 5.22 us -> 3.93 us  [shifted(): return lax.ppermute(x, axis, pairs)]
  transfers between devices with their start and end apart: 4 -> 1, of which waited for: 2 -> 0; matrix products, arithmetic and copies ran while one was open for 4% -> 3% of each run, Pallas kernels for 61% -> 0%
where the time goes in v3:
time: 172 us; the launch traced here: 170 us
  Pallas kernels  156 us (91%)
  local copies, waits for them, and re-layouts  10 us (6%)
  starting transfers between devices  3.93 us (2%)
    pallas_call x1, Pallas kernels, layer(): pl.pallas_call(functools.partial(layer_kernel, zn, blocks), out_shape=[ja...  156 us
    ppermute x1, starting transfers between devices, shifted(): return lax.ppermute(x, axis, pairs)  3.93 us
    reshape x2, local copies, waits for them, and re-layouts, local(): neighbour_values.reshape(rows, length, groups, GROUP, HEAD)  3.65 us
  transfers between devices with their start and end apart: 1, of which 0 were waited for; matrix products, arithmetic and copies ran while one was open for 3% of the time, Pallas kernels for 0%

profile of v3, /device:TPU:1, one launch (start us, length us, event | category | flops | bytes accessed | tf_op | source)
XLA Modules:
  0.0 170.3 jit_solution(12661027210500628895)
XLA Ops:
  0.6 0.0 copy-start.3
  0.6 0.0 copy-start.2
  0.6 0.7 slice.6
  1.4 3.9 %collective-permute-start = (bf16[1,512]{1,0:T(2,128)(2,1)S(1)}, bf16[1,512]{1,0:T(2,128)(2,1)S(1)}, u32[]{:S(2)}, u32[]{:S(2)}) collective-permute-start(bf16[1,512]{1,0:T(2,128)(2,1)S(1)} %slice.6), channel_id=1, source_target_pairs={{0,8},{8,16},{16,24},{24,32},{32,40},{40,48},{48,56},{56,64},{64,7... | collective-permute-start | bytes 3080 | tf_op jit(solution)/shard_map/ppermute | solution.py:38
  5.3 0.0 copy-done.3
  5.3 0.0 copy-done.2
  5.3 1.3 reshape.28
  6.7 2.3 %copy.20 = bf16[8,128,2,2,128]{1,3,4,2,0:T(2,128)(2,1)S(1)} copy(bf16[8,128,2,2,128]{4,3,2,1,0:T(2,128)(2,1)S(1)} %reshape.28) | data formatting | bytes 2097152 | tf_op jit(solution)/shard_map/reshape | solution.py:606
  9.0 0.0 copy-start
  9.0 1.5 reshape.29.v_ref
  10.5 0.1 copy.18
  10.6 0.1 reshape.25
  10.7 0.6 pad.4.code_ref
  11.3 0.0 collective-permute-done
  11.3 0.0 copy-done
  11.3 0.1 pad_maximum_fusion
  11.4 0.1 reshape.26
  11.5 0.9 copy.21.q_ref
  12.3 155.6 %shard_map.113 = (bf16[32,4096]{1,0:T(8,128)(2,1)}, bf16[32,4096]{1,0:T(8,128)(2,1)}) custom-call(s32[8,128]{1,0:T(8,128)} %pad.4.code_ref, bf16[2,4,128,128]{3,2,1,0:T(8,128)(2,1)} %copy.21.q_ref, bf16[8,128,512]{2,1,0:T(8,128)(2,1)} %k_ref.1, bf16[8,2,128,256]{3,2,1,0:T(8,128)(2,1)} %reshape.29.v_ref, bf16[64,512]{1,0:T(8,128)(2,1)} %bitcast.11, ...), custom_call_target="tpu_custom_call" | custom-call | flops 2200000000 | bytes 6000000 | tf_op jit(solution)/shard_map/pallas_call | solution.py:531
  167.9 0.0 copy-start.1
  167.9 1.7 %copy.24 = bf16[32,4096]{1,0:T(8,128)(2,1)} copy(bf16[32,4096]{1,0:T(8,128)(2,1)} %get-tuple-element.4) | data formatting | bytes 524288
  169.6 0.0 copy-done.1
  169.6 0.7 copy.25
  (2 shorter events, 0.1 us)
Async XLA Ops:
  0.6 4.7 %copy-start.3 = (s32[4,2]{0,1:T(2,128)S(1)}, s32[4,2]{0,1:T(2,128)}, u32[]{:S(2)}) copy-start(s32[4,2]{0,1:T(2,128)} %param.18) | copy-start | bytes 100
  0.6 4.7 %copy-start.2 = (s32[4,2]{0,1:T(2,128)S(1)}, s32[4,2]{0,1:T(2,128)}, u32[]{:S(2)}) copy-start(s32[4,2]{0,1:T(2,128)} %param.19) | copy-start | bytes 100
  1.4 9.9 %collective-permute-start = (bf16[1,512]{1,0:T(2,128)(2,1)S(1)}, bf16[1,512]{1,0:T(2,128)(2,1)S(1)}, u32[]{:S(2)}, u32[]{:S(2)}) collective-permute-start(bf16[1,512]{1,0:T(2,128)(2,1)S(1)} %slice.6), channel_id=1, source_target_pairs={{0,8},{8,16},{16,24},{24,32},{32,40},{40,48},{48,56},{56,64},{64,7... | collective-permute-start | bytes 3080 | tf_op jit(solution)/shard_map/ppermute | solution.py:38
  9.0 2.3 %copy-start = (bf16[256,512]{1,0:T(8,128)(2,1)S(1)}, bf16[256,512]{1,0:T(8,128)(2,1)}, u32[]{:S(2)}) copy-start(bf16[256,512]{1,0:T(8,128)(2,1)} %param.10) | copy-start | bytes 786436
  167.9 1.7 %copy-start.1 = (bf16[32,4096]{1,0:T(8,128)(2,1)S(1)}, bf16[32,4096]{1,0:T(8,128)(2,1)}, u32[]{:S(2)}) copy-start(bf16[32,4096]{1,0:T(8,128)(2,1)} %get-tuple-element.5) | copy-start | bytes 786436

commit v4 on v3

--- a/solution.py
+++ b/solution.py
@@ -91,7 +91,7 @@
         rs_recv,
         table_sem,
         weight,
-        merged,
+        own_stat,
         rows_f32,
         sums,
         a_out,
@@ -112,12 +112,13 @@
         b_recv,
     ) = scratch[groups * per_g :]
     far, near = zn // 2, zn // 2 - 1
+    hb = blocks // 2
     chains = [
-        (way, b, far if (b < blocks // 2) == (way > 0) else near)
-        for b in range(blocks)
+        (way, half, far if (half == 0) == (way > 0) else near)
+        for half in range(2)
         for way in (1, -1)
     ]
-    started = []
+    started, pending = [], {}
 
     barrier = pltpu.get_barrier_semaphore()
     for peer in (z_up, z_dn, x_up, x_dn, d_next, d_prev):
@@ -136,10 +137,15 @@
             device_id_type=MESH,
         )
 
-    def remote(src, dst, send, recv, peer):
+    def remote(src, dst, send, recv, peer, key=None):
         copy = copy_to(src, dst, send, recv, peer)
+        if key in pending:
+            pending.pop(key).wait_send()
         copy.start()
-        started.append(copy)
+        if key is None:
+            started.append(copy)
+        else:
+            pending[key] = copy
         return copy
 
     def stores(g):
@@ -149,14 +155,14 @@
         pairs = [(k_ref, bufs[g][1]), (v_ref, bufs[g][2])]
         own, first, later = [], [], []
         for n, (src, dst) in enumerate(pairs):
-            whole = src.at[:, :, cols] if n == 0 else src.at[:, g]
+            whole = src.at[:, :, cols] if n == 0 else src.at[:, cols]
             copy = pltpu.make_async_copy(whole, dst.at[0], kv_own.at[g, n])
             copy.start()
             own.append(copy)
         for part, place, peer, at in ((lo, 3, x_up, 0), (hi, 1, x_dn, 1), (hi, 3, x_up, 2), (lo, 1, x_dn, 3)):
             for n, (src, dst) in enumerate(pairs):
                 copy = remote(
-                    src.at[part, :, cols] if n == 0 else src.at[part, g],
+                    src.at[part, :, cols] if n == 0 else src.at[part, cols],
                     dst.at[place, part],
                     kv_send.at[g, n, at],
                     kv_recv.at[g, n, at],
@@ -192,10 +198,10 @@
                 here = codes.at[(z - way * s + zn) % zn]
                 peer = z_up if way > 0 else z_dn
                 if s > 0:
-                    copy_to(here, here, code_send.at[c, s - 1], code_recv.at[c, s - 1], peer).wait_recv()
+                    copy_to(here, here, code_send.at[c, 0], code_recv.at[c, s - 1], peer).wait_recv()
                 if s < steps:
                     src = code_ref if s == 0 else here
-                    remote(src, here, code_send.at[c, s], code_recv.at[c, s], peer)
+                    remote(src, here, code_send.at[c, s % 2], code_recv.at[c, s], peer, ("c", c, s % 2))
             yield
         copy = pltpu.make_async_copy(codes, table, table_sem)
         copy.start()
@@ -225,18 +231,26 @@
         for b in range(blocks):
             col[z * blocks + b] = q_ref[g, b]
         for s in range(far + 1):
-            for c, (way, block, steps) in enumerate(chains):
+            for c, (way, half, steps) in enumerate(chains):
                 if s > steps:
                     continue
-                here = col.at[((z - way * s + zn) % zn) * blocks + block]
+                at = ((z - way * s + zn) % zn) * blocks + half * hb
+                here = col.at[pl.ds(at, hb)]
                 peer = z_up if way > 0 else z_dn
                 if s > 0:
                     copy_to(
-                        here, here, ag_send.at[g, c, s - 1], ag_recv.at[g, c, s - 1], peer
+                        here, here, ag_send.at[g, c, 0], ag_recv.at[g, c, s - 1], peer
                     ).wait_recv()
                 if s < steps:
-                    src = q_ref.at[g, block] if s == 0 else here
-                    remote(src, here, ag_send.at[g, c, s], ag_recv.at[g, c, s], peer)
+                    src = q_ref.at[g, pl.ds(half * hb, hb)] if s == 0 else here
+                    remote(
+                        src,
+                        here,
+                        ag_send.at[g, c, s % 2],
+                        ag_recv.at[g, c, s],
+                        peer,
+                        ("g", g, c, s % 2),
+                    )
             yield
 
     left = lax.broadcasted_iota(jnp.int32, (HEAD, GROUP * span), 1) < span
@@ -260,66 +274,93 @@
             for r, a, e, top, total in zip(places, at, raised, tops, totals):
                 eb = e.astype(jnp.bfloat16)
                 p2 = jnp.concatenate([eb * left_bf, eb * right_bf], axis=0)
-                part = jnp.dot(values[r, a], p2, preferred_element_type=jnp.float32)
+                v = values[r, a]
+                v2 = jnp.concatenate([v[:HEAD], v[HEAD:]], axis=1)
+                part = jnp.dot(v2, p2, preferred_element_type=jnp.float32)
                 res[z0 * XN + r] = (part * (1.0 / total)).astype(jnp.bfloat16)
                 stat[z0, r : r + 1, :] = top * scale + jnp.log(total)
         stat[z0, XN : XN + 1, :] = jnp.full((1, GROUP * span), NONE, jnp.float32)
 
-    def combine(g, z0, block, arrived, dst, dst_stat):
-        res, stat = bufs[g][3:5]
-        lses = [ref[...] for _, ref in arrived]
-        vals = [ref[...] for ref, _ in arrived]
+    block_row = lax.broadcasted_iota(jnp.int32, (8, GROUP * span), 0)
+
+    def shares(g, z0, arrived, spare):
+        stat = bufs[g][4]
         for r in range(2):
-            place = slots[z0, 2 * XN + 2 * block + r]
-            lses.append(stat[z0, pl.ds(place, 1), :])
-            vals.append(res[z0 * XN + jnp.minimum(place, XN - 1)])
+            for b in range(blocks):
+                place = slots[z0, 2 * XN + 2 * b + r]
+                own_stat[spare + r, b : b + 1, :] = stat[z0, pl.ds(place, 1), :]
+        lses = arrived + [own_stat[spare], own_stat[spare + 1]]
         top = functools.reduce(jnp.maximum, lses)
         weights = [jnp.exp(v - top) for v in lses]
         total = functools.reduce(jnp.add, weights)
-        if dst_stat is not None:
-            dst_stat[...] = top + jnp.log(total)
-        share = 1.0 / total
-        acc = vals[0].astype(jnp.float32) * (weights[0] * share)
-        for v, w in zip(vals[1:], weights[1:]):
-            acc += v.astype(jnp.float32) * (w * share)
-        dst[...] = acc.astype(jnp.bfloat16)
+        return [w / total for w in weights], top + jnp.log(total)
+
+    def combine(g, z0, block, arrived, weights):
+        res = bufs[g][3]
+        vals = list(arrived)
+        for r in range(2):
+            place = slots[z0, 2 * XN + 2 * block + r]
+            vals.append(res[z0 * XN + jnp.minimum(place, XN - 1)])
+        parts = [
+            v.astype(jnp.float32) * w[block : block + 1] for v, w in zip(vals, weights)
+        ]
+        return functools.reduce(jnp.add, parts).astype(jnp.bfloat16)
 
     def reduce(g):
         ring, ring_stat = bufs[g][5:7]
+        for n in range(4):
+            own_stat[4 * g + n] = jnp.full((8, GROUP * span), NONE, jnp.float32)
         attend(g, (z + far) % zn)
-        for s in range(far + 1):
-            for c, (way, block, steps) in enumerate(chains):
+        for s in range(far):
+            ways = []
+            for w, way in enumerate((1, -1)):
+                peer = z_up if way > 0 else z_dn
+                here = ring_stat.at[w, s]
+                arrived = []
+                if s > 0:
+                    copy_to(
+                        here, here, rs_send.at[g, w, 0], rs_recv.at[g, w, s - 1], peer
+                    ).wait_recv()
+                    arrived = [here[...]]
+                z0 = (z + way * (far - s) + zn) % zn
+                weights, lse = shares(g, z0, arrived, 4 * g + 2 * w)
+                if s == 0:
+                    mine = (block_row < hb) == (way > 0)
+                    lse = jnp.where(mine, lse, NONE)
+                here[...] = lse
+                remote(
+                    here,
+                    ring_stat.at[w, s + 1],
+                    rs_send.at[g, w, s % 2],
+                    rs_recv.at[g, w, s],
+                    peer,
+                    ("s", g, w, s % 2),
+                )
+                ways.append((z0, weights))
+            for c, (way, half, steps) in enumerate(chains):
                 i = s - (far - steps)
-                if i < 0 or i > steps:
+                if i < 0:
                     continue
-                here, here_stat = ring.at[c, i], ring_stat.at[c, i, pl.ds(0, 1)]
+                here = ring.at[c, i]
                 peer = z_up if way > 0 else z_dn
+                z0, weights = ways[0 if way > 0 else 1]
                 if i > 0:
-                    for ref, snd, rcv in (
-                        (here, rd_send, rd_recv),
-                        (here_stat, rs_send, rs_recv),
-                    ):
-                        copy_to(
-                            ref, ref, snd.at[g, c, i - 1], rcv.at[g, c, i - 1], peer
-                        ).wait_recv()
-                if i < steps:
-                    z0 = (z + way * (steps - i) + zn) % zn
-                    arrived = [(here, here_stat)] if i > 0 else []
-                    combine(g, z0, block, arrived, here, here_stat)
-                    remote(
-                        here_stat,
-                        ring_stat.at[c, i + 1, pl.ds(0, 1)],
-                        rs_send.at[g, c, i],
-                        rs_recv.at[g, c, i],
-                        peer,
+                    copy_to(
+                        here, here, rd_send.at[g, c, 0], rd_recv.at[g, c, i - 1], peer
+                    ).wait_recv()
+                for b in range(hb):
+                    arrived = [here[b]] if i > 0 else []
+                    here[b] = combine(
+                        g, z0, half * hb + b, arrived, weights[len(weights) - 2 - len(arrived) :]
                     )
-                    remote(
-                        here,
-                        ring.at[c, i + 1],
-                        rd_send.at[g, c, i],
-                        rd_recv.at[g, c, i],
-                        peer,
-                    )
+                remote(
+                    here,
+                    ring.at[c, i + 1],
+                    rd_send.at[g, c, i % 2],
+                    rd_recv.at[g, c, i],
+                    peer,
+                    ("d", g, c, i % 2),
+                )
             away = far - (s + 1)
             if away > 0:
 
@@ -327,17 +368,28 @@
                 def _(n):
                     attend(g, (z + (1 - 2 * n) * away + zn) % zn)
 
-            elif away == 0:
+            else:
                 attend(g, z)
             yield
+        arrived = []
+        for w, peer in enumerate((z_up, z_dn)):
+            here = ring_stat.at[w, far]
+            copy_to(
+                here, here, rs_send.at[g, w, 0], rs_recv.at[g, w, far - 1], peer
+            ).wait_recv()
+            arrived.append(here[...])
+        weights, _ = shares(g, z, arrived, 4 * g)
+        for c, (way, half, steps) in enumerate(chains):
+            here = ring.at[c, steps]
+            peer = z_up if way > 0 else z_dn
+            copy_to(
+                here, here, rd_send.at[g, c, 0], rd_recv.at[g, c, steps - 1], peer
+            ).wait_recv()
         for b in range(blocks):
-            arrived = [
-                (ring.at[c, steps], ring_stat.at[c, steps, pl.ds(0, 1)])
-                for c, (_, block, steps) in enumerate(chains)
-                if block == b
-            ]
-            combine(g, z, b, arrived, merged.at[g, b], None)
-            turned = jnp.transpose(merged[g, b].astype(jnp.float32))
+            half = b // hb
+            arrived = [ring[2 * half + w, chains[2 * half + w][2], b % hb] for w in range(2)]
+            rows = combine(g, z, b, arrived, weights)
+            turned = jnp.transpose(rows.astype(jnp.float32))
             for h in range(GROUP):
                 at = (g * GROUP + h) * HEAD
                 rows_f32[b * span : (b + 1) * span, at : at + HEAD] = turned[
@@ -364,10 +416,10 @@
                 here = weight.at[(z - way * s + zn) % zn, x]
                 peer = z_up if way > 0 else z_dn
                 if s > 0:
-                    copy_to(here, here, w_send.at[c, s - 1], w_recv.at[c, s - 1], peer).wait_recv()
+                    copy_to(here, here, w_send.at[c, 0], w_recv.at[c, s - 1], peer).wait_recv()
                 if s < steps:
                     src = w_ref if s == 0 else here
-                    remote(src, here, w_send.at[c, s], w_recv.at[c, s], peer)
+                    remote(src, here, w_send.at[c, s % 2], w_recv.at[c, s], peer, ("w", c, s % 2))
             yield
         lo, hi = pl.ds(0, zn // 2), pl.ds(zn // 2, zn // 2)
 
@@ -501,7 +553,7 @@
         for _ in it:
             pass
     project()
-    for copy in started:
+    for copy in started + list(pending.values()):
         copy.wait_send()
 
 
@@ -518,16 +570,17 @@
     per_group = [
         pltpu.VMEM((zn * blocks, deep, wide), bf),
         pltpu.VMEM((XN, rows, k.shape[1], GROUP * HEAD), bf),
-        pltpu.VMEM((XN, rows) + v.shape[2:], bf),
+        pltpu.VMEM((XN, rows, GROUP * HEAD, v.shape[2]), bf),
         pltpu.VMEM((zn * XN, deep, wide), bf),
         pltpu.VMEM((zn, 8, wide), f32),
-        pltpu.VMEM((2 * blocks, steps + 1, deep, wide), bf),
-        pltpu.VMEM((2 * blocks, steps + 1, 8, wide), f32),
+        pltpu.VMEM((4, steps + 1, blocks // 2, deep, wide), bf),
+        pltpu.VMEM((2, steps + 1, 8, wide), f32),
     ]
     dma = pltpu.SemaphoreType.DMA
     vmem = pl.BlockSpec(memory_space=pltpu.VMEM)
     hbm = pl.BlockSpec(memory_space=pl.ANY)
-    ring = dma((groups, 2 * blocks, steps))
+    ring = dma((groups, 4, steps))
+    two = dma((groups, 4, 2))
     return pl.pallas_call(
         functools.partial(layer_kernel, zn, blocks),
         out_shape=[jax.ShapeDtypeStruct(residual.shape, bf)] * 2,
@@ -538,20 +591,20 @@
             pltpu.VMEM((zn, 8, HEAD), jnp.int32),
             pltpu.SMEM((zn, 8, HEAD), jnp.int32),
             pltpu.SMEM((zn, 2 * XN + 2 * blocks), jnp.int32),
+            dma((2, 2)),
             dma((2, steps)),
-            dma((2, steps)),
-            ring,
+            two,
             ring,
             dma((groups, 2)),
             dma((groups, 2, 6)),
             dma((groups, 2, 6)),
+            two,
             ring,
-            ring,
-            ring,
-            ring,
+            dma((groups, 2, 2)),
+            dma((groups, 2, steps)),
             dma,
             pltpu.VMEM((zn, XN) + weight.shape, bf),
-            pltpu.VMEM((groups, blocks, deep, wide), bf),
+            pltpu.VMEM((4 * groups, 8, wide), f32),
             pltpu.VMEM((blocks * span + 8, depth), f32),
             pltpu.VMEM((2 * YN, own, width), f32),
             pltpu.VMEM((CUTS, YN, own, cut), bf),
@@ -560,7 +613,7 @@
             pltpu.VMEM((CUTS, own, cut), bf),
             pltpu.VMEM((CUTS, 2, own, cut), bf),
             pltpu.VMEM((CUTS, 2, own, cut), bf),
-            dma((2, steps)),
+            dma((2, 2)),
             dma((2, steps)),
             dma((6,)),
             dma((6,)),
@@ -602,9 +655,7 @@
     asked = jnp.concatenate([carried, queries[:-1]], axis=0)
     asked = asked.reshape(blocks, span, groups, GROUP, HEAD).transpose(2, 0, 4, 3, 1)
     asked = asked.reshape(groups, blocks, HEAD, GROUP * span)
-    rows, length, _ = neighbour_values.shape
-    values = neighbour_values.reshape(rows, length, groups, GROUP, HEAD).transpose(0, 2, 4, 3, 1)
-    values = values.reshape(rows, groups, HEAD, GROUP * length)
+    values = neighbour_values.transpose(0, 2, 1)
     return tuple(
         layer(
             code,

time: 172 us -> 165 us (0.959)
  Pallas kernels: 156 us -> 151 us
  local copies, waits for them, and re-layouts: 10 us -> 7.19 us
    reshape x3 -> x0, local copies, waits for them, and re-layouts: 5.13 us -> none  [the longest x2 3.65 us: local(): neighbour_values.reshape(rows, length, groups, GROUP, HEAD)]
    pallas_call x1, Pallas kernels: 156 us -> 151 us  [layer(): pl.pallas_call(functools.partial(layer_kernel, zn, blocks), out_shape=[ja...]
    unnamed x10 -> x11, local copies, waits for them, and re-layouts: 2.43 us -> 4.73 us
  transfers between devices with their start and end apart: 1 -> 1, of which waited for: 0 -> 0; matrix products, arithmetic and copies ran while one was open for 3% -> 2% of each run, Pallas kernels for 0% -> 0%
where the time goes in v4:
time: 165 us; the launch traced here: 162 us
  Pallas kernels  151 us (92%)
  local copies, waits for them, and re-layouts  7.19 us (4%)
  starting transfers between devices  3.93 us (2%)
    pallas_call x1, Pallas kernels, layer(): pl.pallas_call(functools.partial(layer_kernel, zn, blocks), out_shape=[ja...  151 us
    unnamed x11, local copies, waits for them, and re-layouts  4.73 us
    ppermute x1, starting transfers between devices, shifted(): return lax.ppermute(x, axis, pairs)  3.93 us
  transfers between devices with their start and end apart: 1, of which 0 were waited for; matrix products, arithmetic and copies ran while one was open for 2% of the time, Pallas kernels for 0%

profile of v4, /device:TPU:1, one launch (start us, length us, event | category | flops | bytes accessed | tf_op | source)
XLA Modules:
  0.0 162.5 jit_solution(7370083131822616817)
XLA Ops:
  0.6 0.0 copy-start.2
  0.6 0.0 copy-start.3
  0.6 0.7 slice.6
  1.4 3.9 %collective-permute-start = (bf16[1,512]{1,0:T(2,128)(2,1)S(1)}, bf16[1,512]{1,0:T(2,128)(2,1)S(1)}, u32[]{:S(2)}, u32[]{:S(2)}) collective-permute-start(bf16[1,512]{1,0:T(2,128)(2,1)S(1)} %slice.6), channel_id=1, source_target_pairs={{0,8},{8,16},{16,24},{24,32},{32,40},{40,48},{48,56},{56,64},{64,7... | collective-permute-start | bytes 3080 | tf_op jit(solution)/shard_map/ppermute | solution.py:38
  5.3 0.0 copy-done.2
  5.3 0.0 copy-done.3
  5.3 0.1 copy.18
  5.4 0.1 reshape.19
  5.5 0.0 copy-start
  5.5 2.3 %copy.20 = bf16[8,128,512]{1,2,0:T(8,128)(2,1)} copy(bf16[8,128,512]{2,1,0:T(8,128)(2,1)} %param.12) | data formatting | bytes 2097152 | tf_op args[2]
  7.8 0.6 pad.4.code_ref
  8.4 0.0 collective-permute-done
  8.4 0.0 copy-done
  8.4 0.1 pad_maximum_fusion
  8.5 0.1 reshape.20
  8.6 0.9 copy.21.q_ref
  9.5 150.6 %shard_map.113 = (bf16[32,4096]{1,0:T(8,128)(2,1)}, bf16[32,4096]{1,0:T(8,128)(2,1)}) custom-call(s32[8,128]{1,0:T(8,128)} %pad.4.code_ref, bf16[2,4,128,128]{3,2,1,0:T(8,128)(2,1)} %copy.21.q_ref, bf16[8,128,512]{2,1,0:T(8,128)(2,1)} %k_ref.1, bf16[8,512,128]{2,1,0:T(8,128)(2,1)} %bitcast.7, bf16[64,512]{1,0:T(8,128)(2,1)} %bitcast.11, ...), custom_call_target="tpu_custom_call" | custom-call | flops 2200000000 | bytes 6000000 | tf_op jit(solution)/shard_map/pallas_call | solution.py:584
  160.1 0.0 copy-start.1
  160.1 1.7 %copy.24 = bf16[32,4096]{1,0:T(8,128)(2,1)} copy(bf16[32,4096]{1,0:T(8,128)(2,1)} %get-tuple-element.4) | data formatting | bytes 524288
  161.8 0.0 copy-done.1
  161.8 0.7 copy.25
  (2 shorter events, 0.1 us)
Async XLA Ops:
  0.6 4.7 %copy-start.2 = (s32[4,2]{0,1:T(2,128)S(1)}, s32[4,2]{0,1:T(2,128)}, u32[]{:S(2)}) copy-start(s32[4,2]{0,1:T(2,128)} %param.19) | copy-start | bytes 100
  0.6 4.7 %copy-start.3 = (s32[4,2]{0,1:T(2,128)S(1)}, s32[4,2]{0,1:T(2,128)}, u32[]{:S(2)}) copy-start(s32[4,2]{0,1:T(2,128)} %param.18) | copy-start | bytes 100
  1.4 7.1 %collective-permute-start = (bf16[1,512]{1,0:T(2,128)(2,1)S(1)}, bf16[1,512]{1,0:T(2,128)(2,1)S(1)}, u32[]{:S(2)}, u32[]{:S(2)}) collective-permute-start(bf16[1,512]{1,0:T(2,128)(2,1)S(1)} %slice.6), channel_id=1, source_target_pairs={{0,8},{8,16},{16,24},{24,32},{32,40},{40,48},{48,56},{56,64},{64,7... | collective-permute-start | bytes 3080 | tf_op jit(solution)/shard_map/ppermute | solution.py:38
  5.5 2.9 %copy-start = (bf16[256,512]{1,0:T(8,128)(2,1)S(1)}, bf16[256,512]{1,0:T(8,128)(2,1)}, u32[]{:S(2)}) copy-start(bf16[256,512]{1,0:T(8,128)(2,1)} %param.10) | copy-start | bytes 786436
  160.1 1.7 %copy-start.1 = (bf16[32,4096]{1,0:T(8,128)(2,1)S(1)}, bf16[32,4096]{1,0:T(8,128)(2,1)}, u32[]{:S(2)}) copy-start(bf16[32,4096]{1,0:T(8,128)(2,1)} %get-tuple-element.5) | copy-start | bytes 786436

commit v5 on v4

--- a/solution.py
+++ b/solution.py
@@ -24,18 +24,14 @@
     + [("w", "c", "g0", "g1")] * 3
     + [("w", "c", "c", "g0", "g1"), ("k0",)]
     + [("w", "r0")] * 3
-    + [("k1", "w", "r0"), ("w", "r0"), ("k1", "w", "r0", "r1")]
-    + [("r0", "r1")] * 2
-    + [("w", "r0", "r1"), ("r0", "r1"), ("r1",), ("w",), ("r1",)]
+    + [("k1", "w", "r0"), ("k1", "w", "r0", "r1"), ("w", "r0", "r1")]
+    + [("r0", "r1")] * 3
+    + [("w", "r1")]
+    + [("r1",)] * 3
+    + [("w",), ("r1",)]
 )
 YN = 4
 CUTS = 4
-
-
-def shifted(x, axis, by):
-    count = lax.axis_size(axis)
-    pairs = [(i, i + by) for i in range(count) if 0 <= i + by < count]
-    return lax.ppermute(x, axis, pairs)
 
 
 def layer_kernel(
@@ -54,8 +50,9 @@
     normed_ref,
     *scratch,
 ):
-    groups = q_ref.shape[0]
-    span = q_ref.shape[3] // GROUP
+    total = q_ref.shape[0]
+    span = total // blocks
+    groups = q_ref.shape[1] // (GROUP * HEAD)
     wide = GROUP * HEAD
     rows = k_ref.shape[0]
     me = lax.axis_index("dp")
@@ -110,6 +107,11 @@
         a_recv,
         b_send,
         b_recv,
+        q_f32,
+        v_here,
+        q_send,
+        q_recv,
+        v_sem,
     ) = scratch[groups * per_g :]
     far, near = zn // 2, zn // 2 - 1
     hb = blocks // 2
@@ -125,6 +127,14 @@
         pl.semaphore_signal(barrier, inc=1, device_id=(peer, tens), device_id_type=MESH)
     for peer in (y_up, y_dn, partner):
         pl.semaphore_signal(barrier, inc=1, device_id=(me, peer), device_id_type=MESH)
+    v_copies = []
+    for g in range(groups):
+        copy = pltpu.make_async_copy(
+            v_ref.at[:, :, pl.ds(g * wide, wide)], v_here.at[g], v_sem.at[g]
+        )
+        copy.start()
+        v_copies.append(copy)
+    q_f32[8:, :] = q_ref[...].astype(jnp.float32)
     pl.semaphore_wait(barrier, 9)
 
     def copy_to(src, dst, send, recv, peer):
@@ -152,41 +162,37 @@
         hb = rows // 2
         lo, hi = pl.ds(0, hb), pl.ds(hb, hb)
         cols = pl.ds(g * wide, wide)
-        pairs = [(k_ref, bufs[g][1]), (v_ref, bufs[g][2])]
-        own, first, later = [], [], []
-        for n, (src, dst) in enumerate(pairs):
-            whole = src.at[:, :, cols] if n == 0 else src.at[:, cols]
-            copy = pltpu.make_async_copy(whole, dst.at[0], kv_own.at[g, n])
-            copy.start()
-            own.append(copy)
-        for part, place, peer, at in ((lo, 3, x_up, 0), (hi, 1, x_dn, 1), (hi, 3, x_up, 2), (lo, 1, x_dn, 3)):
-            for n, (src, dst) in enumerate(pairs):
-                copy = remote(
-                    src.at[part, :, cols] if n == 0 else src.at[part, cols],
-                    dst.at[place, part],
-                    kv_send.at[g, n, at],
-                    kv_recv.at[g, n, at],
-                    peer,
-                )
-                (first if at < 2 else later).append(copy)
+        keys, values = bufs[g][1:3]
+        routes = ((lo, 3, x_up, 0), (hi, 1, x_dn, 1), (hi, 3, x_up, 2), (lo, 1, x_dn, 3))
+        copies = {}
+
+        def send(n, at, src, dst, peer):
+            copies[n, at] = remote(src, dst, kv_send.at[g, n, at], kv_recv.at[g, n, at], peer)
+
+        own = pltpu.make_async_copy(k_ref.at[:, :, cols], keys.at[0], kv_own.at[g])
+        own.start()
+        for part, place, peer, at in routes:
+            send(0, at, k_ref.at[part, :, cols], keys.at[place, part], peer)
+        v_copies[g].wait()
+
+        @pl.loop(0, rows)
+        def _(n):
+            for h in range(GROUP):
+                here = slice(h * HEAD, (h + 1) * HEAD)
+                values[0, n, here, :] = jnp.transpose(v_here[g, n, :, here])
+
+        for part, place, peer, at in routes:
+            send(1, at, values.at[0, part], values.at[place, part], peer)
         yield
-        for i, (part, place, peer, at) in enumerate(((lo, 3, x_up, 4), (hi, 1, x_dn, 5))):
-            for n, (_, dst) in enumerate(pairs):
-                first[2 * i + n].wait_recv()
-                later.append(
-                    remote(
-                        dst.at[place, part],
-                        dst.at[2, part],
-                        kv_send.at[g, n, at],
-                        kv_recv.at[g, n, at],
-                        peer,
-                    )
-                )
+        for part, place, peer, at in ((lo, 3, x_up, 0), (hi, 1, x_dn, 1)):
+            for n, buf in enumerate((keys, values)):
+                copies[n, at].wait_recv()
+                send(n, at + 4, buf.at[place, part], buf.at[2, part], peer)
         yield
-        for copy in own:
-            copy.wait()
-        for copy in later:
-            copy.wait_recv()
+        own.wait()
+        for n in range(2):
+            for at in range(2, 6):
+                copies[n, at].wait_recv()
         yield
 
     def gather_codes():
@@ -226,25 +232,46 @@
 
         yield
 
+    def own_block(g, b):
+        if b == 0 and q_wait:
+            q_wait.pop().wait_recv()
+        top = 8 + b * span - 1
+        at = g * wide
+        parts = [
+            q_f32[top : top + span, at + h * HEAD : at + (h + 1) * HEAD] for h in range(GROUP)
+        ]
+        turned = jnp.transpose(jnp.concatenate(parts, axis=0))
+        if b == 0:
+            row = lax.broadcasted_iota(jnp.int32, turned.shape, 1) % span
+            turned = jnp.where((row == 0) & (me == 0), 0.0, turned)
+        bufs[g][0][z * blocks + b] = turned.astype(jnp.bfloat16)
+
+    q_wait = [
+        remote(
+            q_f32.at[pl.ds(total, 8)], q_f32.at[pl.ds(0, 8)], q_send, q_recv, d_next
+        )
+    ]
+
     def gather(g):
         col = bufs[g][0]
-        for b in range(blocks):
-            col[z * blocks + b] = q_ref[g, b]
         for s in range(far + 1):
-            for c, (way, half, steps) in enumerate(chains):
+            for c, (way, half, steps) in enumerate(chains[::-1] if s == 0 else chains):
+                c = len(chains) - 1 - c if s == 0 else c
                 if s > steps:
                     continue
                 at = ((z - way * s + zn) % zn) * blocks + half * hb
                 here = col.at[pl.ds(at, hb)]
                 peer = z_up if way > 0 else z_dn
+                if s == 0 and c % 2 == 1:
+                    for b in range(half * hb, (half + 1) * hb):
+                        own_block(g, b)
                 if s > 0:
                     copy_to(
                         here, here, ag_send.at[g, c, 0], ag_recv.at[g, c, s - 1], peer
                     ).wait_recv()
                 if s < steps:
-                    src = q_ref.at[g, pl.ds(half * hb, hb)] if s == 0 else here
                     remote(
-                        src,
+                        here,
                         here,
                         ag_send.at[g, c, s % 2],
                         ag_recv.at[g, c, s],
@@ -440,7 +467,6 @@
         yield
 
     def project():
-        total = blocks * span
         width = next_ref.shape[1]
         depth = rows_f32.shape[1]
         own = total // (2 * YN)
@@ -557,20 +583,21 @@
         copy.wait_send()
 
 
-def layer(code, q, k, v, weight, residual, drop, gain, bias):
-    groups, blocks, deep, wide = q.shape
+def layer(blocks, code, q, k, v, weight, residual, drop, gain, bias):
+    total, depth = q.shape
+    groups = depth // (GROUP * HEAD)
+    span = total // blocks
+    deep, wide = HEAD, GROUP * span
     rows = k.shape[0]
     zn = lax.axis_size("dp") // XN
     steps = zn // 2
     bf, f32 = jnp.bfloat16, jnp.float32
     own, width = residual.shape
-    depth = weight.shape[1]
     cut = width // CUTS
-    span = wide // GROUP
     per_group = [
         pltpu.VMEM((zn * blocks, deep, wide), bf),
         pltpu.VMEM((XN, rows, k.shape[1], GROUP * HEAD), bf),
-        pltpu.VMEM((XN, rows, GROUP * HEAD, v.shape[2]), bf),
+        pltpu.VMEM((XN, rows, GROUP * HEAD, v.shape[1]), bf),
         pltpu.VMEM((zn * XN, deep, wide), bf),
         pltpu.VMEM((zn, 8, wide), f32),
         pltpu.VMEM((4, steps + 1, blocks // 2, deep, wide), bf),
@@ -595,7 +622,7 @@
             dma((2, steps)),
             two,
             ring,
-            dma((groups, 2)),
+            dma((groups,)),
             dma((groups, 2, 6)),
             dma((groups, 2, 6)),
             two,
@@ -623,6 +650,11 @@
             dma((CUTS,)),
             dma((CUTS, 6)),
             dma((CUTS, 6)),
+            pltpu.VMEM((8 + total, depth), f32),
+            pltpu.VMEM((groups, rows, v.shape[1], GROUP * HEAD), bf),
+            dma,
+            dma,
+            dma((groups,)),
         ],
         compiler_params=pltpu.CompilerParams(
             collective_id=0, has_side_effects=True, vmem_limit_bytes=56 * 1024 * 1024
@@ -645,23 +677,16 @@
     neighbour_owner,
     neighbour_slot,
 ):
-    row_width = queries.shape[1]
     blocks = neighbour_owner.shape[0]
-    span = queries.shape[0] // blocks
-    groups = row_width // (GROUP * HEAD)
     code = (neighbour_owner * neighbour_keys.shape[0] + neighbour_slot).reshape(1, -1)
     code = jnp.pad(code, ((0, 7), (0, HEAD - code.shape[1])))
-    carried = shifted(queries[-1:], "dp", 1)
-    asked = jnp.concatenate([carried, queries[:-1]], axis=0)
-    asked = asked.reshape(blocks, span, groups, GROUP, HEAD).transpose(2, 0, 4, 3, 1)
-    asked = asked.reshape(groups, blocks, HEAD, GROUP * span)
-    values = neighbour_values.transpose(0, 2, 1)
     return tuple(
         layer(
+            blocks,
             code,
-            asked,
+            queries,
             neighbour_keys,
-            values,
+            neighbour_values,
             out_weight.T,
             residual,
             drop_mask,

time: 165 us -> 157 us (0.952)
  starting transfers between devices: 3.93 us -> 0 us
  local copies, waits for them, and re-layouts: 7.19 us -> 3.88 us
    ppermute x1 -> x0, starting transfers between devices: 3.93 us -> none  [shifted(): return lax.ppermute(x, axis, pairs)]
    unnamed x11 -> x8, local copies, waits for them, and re-layouts: 4.73 us -> 3.1 us
  transfers between devices with their start and end apart: 1 -> 0, of which waited for: 0 -> 0; matrix products, arithmetic and copies ran while one was open for 2% -> 0% of each run, Pallas kernels for 0% -> 0%
where the time goes in v5:
time: 157 us; the launch traced here: 155 us
  Pallas kernels  151 us (96%)
  local copies, waits for them, and re-layouts  3.88 us (2%)
    pallas_call x1, Pallas kernels, layer(): pl.pallas_call(functools.partial(layer_kernel, zn, blocks), out_shape=[ja...  151 us

profile of v5, /device:TPU:1, one launch (start us, length us, event | category | flops | bytes accessed | tf_op | source)
XLA Modules:
  0.0 155.1 jit_solution(17821203019510166766)
XLA Ops:
  0.6 0.0 copy-start.2
  0.6 0.0 copy-start.1
  0.6 0.7 copy-done.2
  1.3 0.0 copy-done.1
  1.3 0.1 copy.13
  1.4 0.1 reshape.13
  1.5 0.6 pad.4.code_ref
  2.1 150.6 %shard_map.113 = (bf16[32,4096]{1,0:T(8,128)(2,1)}, bf16[32,4096]{1,0:T(8,128)(2,1)}) custom-call(s32[8,128]{1,0:T(8,128)} %pad.4.code_ref, bf16[256,512]{1,0:T(8,128)(2,1)} %q_ref.1, bf16[8,128,512]{2,1,0:T(8,128)(2,1)} %k_ref.1, bf16[8,128,512]{2,1,0:T(8,128)(2,1)} %v_ref.1, bf16[64,512]{1,0:T(8,128)(2,1)} %bitcast.3, bf16[32,4096]{1,0:T(8,128)(2,1)} %residual_ref.1, ...), custom_call_target="tpu_custom_call" | custom-call | flops 2200000000 | bytes 6000000 | tf_op jit(solution)/shard_map/pallas_call | solution.py:611
  152.7 0.0 copy-start
  152.7 1.7 %copy.16 = bf16[32,4096]{1,0:T(8,128)(2,1)} copy(bf16[32,4096]{1,0:T(8,128)(2,1)} %get-tuple-element.4) | data formatting | bytes 524288
  154.4 0.0 copy-done
  154.4 0.7 copy.17
  (1 shorter events, 0.0 us)
Async XLA Ops:
  0.6 0.7 copy-start.2
  0.6 0.7 copy-start.1
  152.7 1.7 %copy-start = (bf16[32,4096]{1,0:T(8,128)(2,1)S(1)}, bf16[32,4096]{1,0:T(8,128)(2,1)}, u32[]{:S(2)}) copy-start(bf16[32,4096]{1,0:T(8,128)(2,1)} %get-tuple-element.5) | copy-start | bytes 786436

commit v6 on v5

--- a/solution.py
+++ b/solution.py
@@ -31,19 +31,20 @@
     + [("w",), ("r1",)]
 )
 YN = 4
-CUTS = 4
+CUTS = 2
 
 
 def layer_kernel(
     zn,
     blocks,
-    code_ref,
+    owner_ref,
+    slot_ref,
     q_ref,
     k_ref,
     v_ref,
     w_ref,
-    residual_ref,
-    drop_ref,
+    residual_hbm,
+    drop_hbm,
     gain_ref,
     bias_ref,
     next_ref,
@@ -112,6 +113,9 @@
         q_send,
         q_recv,
         v_sem,
+        residual_ref,
+        drop_ref,
+        in_sem,
     ) = scratch[groups * per_g :]
     far, near = zn // 2, zn // 2 - 1
     hb = blocks // 2
@@ -134,6 +138,12 @@
         )
         copy.start()
         v_copies.append(copy)
+    late = [
+        pltpu.make_async_copy(residual_hbm, residual_ref, in_sem.at[0]),
+        pltpu.make_async_copy(drop_hbm, drop_ref, in_sem.at[1]),
+    ]
+    for copy in late:
+        copy.start()
     q_f32[8:, :] = q_ref[...].astype(jnp.float32)
     pl.semaphore_wait(barrier, 9)
 
@@ -196,7 +206,8 @@
         yield
 
     def gather_codes():
-        codes[z] = code_ref[...]
+        codes[z] = jnp.zeros(codes.shape[1:], jnp.int32)
+        codes[z, 0:blocks, 0:2] = owner_ref[...] * rows + slot_ref[...]
         for s in range(far + 1):
             for c, (way, steps) in enumerate(((1, far), (-1, near))):
                 if s > steps:
@@ -206,8 +217,7 @@
                 if s > 0:
                     copy_to(here, here, code_send.at[c, 0], code_recv.at[c, s - 1], peer).wait_recv()
                 if s < steps:
-                    src = code_ref if s == 0 else here
-                    remote(src, here, code_send.at[c, s % 2], code_recv.at[c, s], peer, ("c", c, s % 2))
+                    remote(here, here, code_send.at[c, s % 2], code_recv.at[c, s], peer, ("c", c, s % 2))
             yield
         copy = pltpu.make_async_copy(codes, table, table_sem)
         copy.start()
@@ -215,7 +225,7 @@
 
         @pl.loop(0, zn)
         def _(z0):
-            asks = [table[z0, 0, k] for k in range(2 * blocks)]
+            asks = [table[z0, k // 2, k % 2] for k in range(2 * blocks)]
             for r in range(XN):
                 first = (z * XN + (x + r) % XN) * rows
                 block, at = jnp.int32(0), jnp.int32(0)
@@ -308,7 +318,7 @@
                 stat[z0, r : r + 1, :] = top * scale + jnp.log(total)
         stat[z0, XN : XN + 1, :] = jnp.full((1, GROUP * span), NONE, jnp.float32)
 
-    block_row = lax.broadcasted_iota(jnp.int32, (8, GROUP * span), 0)
+    block_row = lax.broadcasted_iota(jnp.int32, (blocks, GROUP * span), 0)
 
     def shares(g, z0, arrived, spare):
         stat = bufs[g][4]
@@ -316,7 +326,7 @@
             for b in range(blocks):
                 place = slots[z0, 2 * XN + 2 * b + r]
                 own_stat[spare + r, b : b + 1, :] = stat[z0, pl.ds(place, 1), :]
-        lses = arrived + [own_stat[spare], own_stat[spare + 1]]
+        lses = arrived + [own_stat[spare + r, 0:blocks, :] for r in range(2)]
         top = functools.reduce(jnp.maximum, lses)
         weights = [jnp.exp(v - top) for v in lses]
         total = functools.reduce(jnp.add, weights)
@@ -335,14 +345,12 @@
 
     def reduce(g):
         ring, ring_stat = bufs[g][5:7]
-        for n in range(4):
-            own_stat[4 * g + n] = jnp.full((8, GROUP * span), NONE, jnp.float32)
         attend(g, (z + far) % zn)
         for s in range(far):
             ways = []
             for w, way in enumerate((1, -1)):
                 peer = z_up if way > 0 else z_dn
-                here = ring_stat.at[w, s]
+                here = ring_stat.at[w, s, pl.ds(0, blocks)]
                 arrived = []
                 if s > 0:
                     copy_to(
@@ -357,7 +365,7 @@
                 here[...] = lse
                 remote(
                     here,
-                    ring_stat.at[w, s + 1],
+                    ring_stat.at[w, s + 1, pl.ds(0, blocks)],
                     rs_send.at[g, w, s % 2],
                     rs_recv.at[g, w, s],
                     peer,
@@ -400,7 +408,7 @@
             yield
         arrived = []
         for w, peer in enumerate((z_up, z_dn)):
-            here = ring_stat.at[w, far]
+            here = ring_stat.at[w, far, pl.ds(0, blocks)]
             copy_to(
                 here, here, rs_send.at[g, w, 0], rs_recv.at[g, w, far - 1], peer
             ).wait_recv()
@@ -422,16 +430,17 @@
                 rows_f32[b * span : (b + 1) * span, at : at + HEAD] = turned[
                     h * span : (h + 1) * span
                 ]
-        cols = pl.ds(g * wide, wide)
-        halo.append(
-            remote(
-                rows_f32.at[pl.ds(0, 8), cols],
-                rows_f32.at[pl.ds(blocks * span, 8), cols],
-                h_send.at[g],
-                h_recv.at[g],
-                d_prev,
-            )
-        )
+            if b == 0:
+                cols = pl.ds(g * wide, wide)
+                halo.append(
+                    remote(
+                        rows_f32.at[pl.ds(0, 8), cols],
+                        rows_f32.at[pl.ds(blocks * span, 8), cols],
+                        h_send.at[g],
+                        h_recv.at[g],
+                        d_prev,
+                    )
+                )
         yield
 
     def gather_weight():
@@ -475,6 +484,8 @@
         half = own // 2
         up, dn, op = (y + 1) % YN, (y + YN - 1) % YN, (y + 2) % YN
         lo, hi = pl.ds(0, half), pl.ds(half, half)
+        for copy in late:
+            copy.wait()
         for copy in halo:
             copy.wait_recv()
         cross = rows_f32[1 : total + 1, :]
@@ -583,8 +594,9 @@
         copy.wait_send()
 
 
-def layer(blocks, code, q, k, v, weight, residual, drop, gain, bias):
+def layer(owner, slot, q, k, v, weight, residual, drop, gain, bias):
     total, depth = q.shape
+    blocks = owner.shape[0]
     groups = depth // (GROUP * HEAD)
     span = total // blocks
     deep, wide = HEAD, GROUP * span
@@ -611,7 +623,7 @@
     return pl.pallas_call(
         functools.partial(layer_kernel, zn, blocks),
         out_shape=[jax.ShapeDtypeStruct(residual.shape, bf)] * 2,
-        in_specs=[vmem, vmem, hbm, hbm] + [vmem] * 5,
+        in_specs=[vmem] * 3 + [hbm, hbm, vmem, hbm, hbm, vmem, vmem],
         out_specs=[vmem, vmem],
         scratch_shapes=per_group * groups
         + [
@@ -655,6 +667,9 @@
             dma,
             dma,
             dma((groups,)),
+            pltpu.VMEM(residual.shape, residual.dtype),
+            pltpu.VMEM(drop.shape, drop.dtype),
+            dma((2,)),
         ],
         compiler_params=pltpu.CompilerParams(
             collective_id=0, has_side_effects=True, vmem_limit_bytes=56 * 1024 * 1024
@@ -662,7 +677,7 @@
         cost_estimate=pl.CostEstimate(
             flops=2_200_000_000, bytes_accessed=6_000_000, transcendentals=2_200_000
         ),
-    )(code, q, k, v, weight, residual, drop, gain, bias)
+    )(owner, slot, q, k, v, weight, residual, drop, gain, bias)
 
 
 def local(
@@ -677,13 +692,10 @@
     neighbour_owner,
     neighbour_slot,
 ):
-    blocks = neighbour_owner.shape[0]
-    code = (neighbour_owner * neighbour_keys.shape[0] + neighbour_slot).reshape(1, -1)
-    code = jnp.pad(code, ((0, 7), (0, HEAD - code.shape[1])))
     return tuple(
         layer(
-            blocks,
-            code,
+            neighbour_owner,
+            neighbour_slot,
             queries,
             neighbour_keys,
             neighbour_values,

time: 157 us -> 155 us (0.987)
  Pallas kernels: 151 us -> 149 us
    unnamed x8 -> x10, local copies, waits for them, and re-layouts: 3.1 us -> 4.43 us
where the time goes in v6:
time: 155 us; the launch traced here: 154 us
  Pallas kernels  149 us (96%)
  local copies, waits for them, and re-layouts  4.43 us (3%)
    pallas_call x1, Pallas kernels, layer(): pl.pallas_call(functools.partial(layer_kernel, zn, blocks), out_shape=[ja...  149 us
    unnamed x10, local copies, waits for them, and re-layouts  4.43 us

profile of v6, /device:TPU:1, one launch (start us, length us, event | category | flops | bytes accessed | tf_op | source)
XLA Modules:
  0.0 154.4 jit_solution(10150192005025864497)
XLA Ops:
  0.6 0.0 copy-start.1
  0.6 0.7 copy-done.1
  1.3 0.0 copy-start.2
  1.3 0.7 copy.12.owner_ref
  2.0 0.0 copy-done.2
  2.0 0.7 copy.13.slot_ref
  2.7 149.3 %shard_map.113 = (bf16[32,4096]{1,0:T(8,128)(2,1)}, bf16[32,4096]{1,0:T(8,128)(2,1)}) custom-call(s32[4,2]{1,0:T(4,128)} %copy.12.owner_ref, s32[4,2]{1,0:T(4,128)} %copy.13.slot_ref, bf16[256,512]{1,0:T(8,128)(2,1)} %q_ref.1, bf16[8,128,512]{2,1,0:T(8,128)(2,1)} %k_ref.1, bf16[8,128,512]{2,1,0:T(8,128)(2,1)} %v_ref.1, bf16[64,512]{1,0:T(8,128)(2,1)} %bitcast.3, ...), custom_call_target="tpu_custom_call" | custom-call | flops 2200000000 | bytes 6000000 | tf_op jit(solution)/shard_map/pallas_call | solution.py:623
  151.9 0.0 copy-start
  151.9 1.7 %copy.16 = bf16[32,4096]{1,0:T(8,128)(2,1)} copy(bf16[32,4096]{1,0:T(8,128)(2,1)} %get-tuple-element.4) | data formatting | bytes 524288
  153.6 0.0 copy-done
  153.6 0.7 copy.17
Async XLA Ops:
  0.6 0.7 copy-start.1
  1.3 0.7 copy-start.2
  151.9 1.7 %copy-start = (bf16[32,4096]{1,0:T(8,128)(2,1)S(1)}, bf16[32,4096]{1,0:T(8,128)(2,1)}, u32[]{:S(2)}) copy-start(bf16[32,4096]{1,0:T(8,128)(2,1)} %get-tuple-element.5) | copy-start | bytes 786436

commit v7 on v6

--- a/solution.py
+++ b/solution.py
@@ -21,12 +21,12 @@
     [("k0", "c", "g0", "g1")]
     + [("c", "g0", "g1")] * 3
     + [("c", "g0", "g1", "k0", "k1")]
-    + [("w", "c", "g0", "g1")] * 3
-    + [("w", "c", "c", "g0", "g1"), ("k0",)]
-    + [("w", "r0")] * 3
-    + [("k1", "w", "r0"), ("k1", "w", "r0", "r1"), ("w", "r0", "r1")]
+    + [("c", "g0", "g1", "w")] * 3
+    + [("c", "c", "g0", "g1", "w"), ("k0",)]
+    + [("r0", "w")] * 3
+    + [("k1", "r0", "w"), ("k1", "r0", "r1", "w"), ("r0", "r1", "w")]
     + [("r0", "r1")] * 3
-    + [("w", "r1")]
+    + [("r1", "w")]
     + [("r1",)] * 3
     + [("w",), ("r1",)]
 )

time: 155 us -> 153 us (0.987)
  Pallas kernels: 149 us -> 147 us
    pallas_call x1, Pallas kernels: 149 us -> 147 us  [layer(): pl.pallas_call(functools.partial(layer_kernel, zn, blocks), out_shape=[ja...]
where the time goes in v7:
time: 153 us; the launch traced here: 152 us
  Pallas kernels  147 us (96%)
  local copies, waits for them, and re-layouts  4.43 us (3%)
    pallas_call x1, Pallas kernels, layer(): pl.pallas_call(functools.partial(layer_kernel, zn, blocks), out_shape=[ja...  147 us
    unnamed x10, local copies, waits for them, and re-layouts  4.43 us

profile of v7, /device:TPU:1, one launch (start us, length us, event | category | flops | bytes accessed | tf_op | source)
XLA Modules:
  0.0 152.4 jit_solution(17873411526739446538)
XLA Ops:
  0.6 0.0 copy-start.1
  0.6 0.7 copy-done.1
  1.3 0.0 copy-start.2
  1.3 0.7 copy.12.owner_ref
  2.0 0.0 copy-done.2
  2.0 0.7 copy.13.slot_ref
  2.7 147.4 %shard_map.113 = (bf16[32,4096]{1,0:T(8,128)(2,1)}, bf16[32,4096]{1,0:T(8,128)(2,1)}) custom-call(s32[4,2]{1,0:T(4,128)} %copy.12.owner_ref, s32[4,2]{1,0:T(4,128)} %copy.13.slot_ref, bf16[256,512]{1,0:T(8,128)(2,1)} %q_ref.1, bf16[8,128,512]{2,1,0:T(8,128)(2,1)} %k_ref.1, bf16[8,128,512]{2,1,0:T(8,128)(2,1)} %v_ref.1, bf16[64,512]{1,0:T(8,128)(2,1)} %bitcast.3, ...), custom_call_target="tpu_custom_call" | custom-call | flops 2200000000 | bytes 6000000 | tf_op jit(solution)/shard_map/pallas_call | solution.py:623
  150.0 0.0 copy-start
  150.0 1.7 %copy.16 = bf16[32,4096]{1,0:T(8,128)(2,1)} copy(bf16[32,4096]{1,0:T(8,128)(2,1)} %get-tuple-element.4) | data formatting | bytes 524288
  151.7 0.0 copy-done
  151.7 0.7 copy.17
Async XLA Ops:
  0.6 0.7 copy-start.1
  1.3 0.7 copy-start.2
  150.0 1.7 %copy-start = (bf16[32,4096]{1,0:T(8,128)(2,1)S(1)}, bf16[32,4096]{1,0:T(8,128)(2,1)}, u32[]{:S(2)}) copy-start(bf16[32,4096]{1,0:T(8,128)(2,1)} %get-tuple-element.5) | copy-start | bytes 786436
